TPU v7x, 32 devices: a whole 2x2x4 slice. The times are simulated.
32 devices in a mesh: groups: 2 (over x), row: 16 (over z, y, core).
Axes of the slice: x: 2, y: 2, z: 4, core: 2. Of those that a mesh axis runs over, the one named last changes fastest.
Arguments:
- tiles: bfloat16 [2048, 128, 128], P(('groups', 'row')), parts along dimension 0, may hold values from -0.41992188 to 0.41992188
- tile_row: int32 [2048, 1], P(('groups', 'row')), parts along dimension 0, may hold values from 0 to 63; in each aligned block of 64 rows (0 to 63, 64 to 127, ...) at most 2 rows name the same one
- tile_col: int32 [2048, 1], P(('groups', 'row')), parts along dimension 0, may hold values from 0 to 63; in each aligned block of 64 rows (0 to 63, 64 to 127, ...) at most 2 rows name the same one
- tile_aux: int32 [2048], P(('groups', 'row')), parts along dimension 0, may hold values from 0 to 15
- coeffs: bfloat16 [16384, 1024], P(('groups', 'row')), parts along dimension 0, may hold values from -0.5 to 0.5
Outputs:
- pair_ints: float32 [32, 96, 1024], P('groups', None, 'row'), parts along dimension 0
There are 2 independent parts, one for each index of `groups`. A program takes and returns all parts, laid end to end along the dimension named above; each array names one. Nothing has to cross between parts.
Inputs may be any that keep to these rules, and one draw needn't show every extreme that they name: `tile_row`: in the rows of one builder (aligned blocks of 64 tiles) no row block is named by more than 2 tiles; some row block is named by exactly 2. `tile_col`: in the rows of one builder (aligned blocks of 64 tiles) no column block is named by more than 2 tiles; some column block is named by exactly 2.
All inputs are finite; a program needn't handle non-finite values.
Results may differ from a plain program's by a relative error of at most 0.005.
Values may be sent and summed in bfloat16 or wider, within the bound.
A program may use at most 128 MiB of HBM per device.

v0:
```python
import jax
import jax.numpy as jnp
from jax import lax
from jax.sharding import PartitionSpec as P

OI = 96
AUX = 16
CAP = 2


def pack_for(tiles, target, auxes, rows, cols, peers, per_peer, naux):
    count = target.shape[0]
    order = jnp.arange(count, dtype=jnp.int32)
    same = target[:, None] == target[None, :]
    before = order[None, :] < order[:, None]
    rank = jnp.sum(jnp.logical_and(same, before), axis=1)
    slot = target * per_peer + rank
    wanted = jnp.arange(peers * per_peer, dtype=jnp.int32)
    hit = slot[:, None] == wanted[None, :]
    filled = jnp.any(hit, axis=0)
    picker = hit.astype(tiles.dtype)
    packed = jnp.einsum("ts,tnm->snm", picker, tiles, preferred_element_type=jnp.float32).astype(
        tiles.dtype
    )
    aux_pick = jnp.sum(jnp.where(hit, auxes[:, None], 0), axis=0)
    row_pick = jnp.sum(jnp.where(hit, rows[:, None], 0), axis=0)
    col_pick = jnp.sum(jnp.where(hit, cols[:, None], 0), axis=0)
    aux_out = jnp.where(filled, aux_pick, naux)
    return (packed, aux_out, row_pick, col_pick)


def select_blocks(table, index):
    choices_at = jnp.arange(table.shape[0], dtype=jnp.int32)
    picker = (index[:, None] == choices_at[None, :]).astype(table.dtype)
    return jnp.einsum("sb,bnj->snj", picker, table, preferred_element_type=jnp.float32).astype(
        table.dtype
    )


def contract(got, got_aux, left_index, right_index, left_table, right_table, naux):
    slots = got.shape[0]
    width = 16
    turns = slots // width
    tile = got.shape[1]
    pieces = got.reshape(turns, width, tile, tile)
    auxes = got_aux.reshape(turns, width)
    lefts_at = left_index.reshape(turns, width)
    rights_at = right_index.reshape(turns, width)
    start = jnp.zeros((naux, left_table.shape[2], right_table.shape[2]), jnp.float32)
    aux_ids = jnp.arange(naux, dtype=jnp.int32)

    def step(total, items):
        piece, aux_now, left_now, right_now = items
        lefts = jnp.einsum(
            "snq,snm->sqm",
            select_blocks(left_table, left_now),
            piece,
            preferred_element_type=jnp.float32,
        ).astype(jnp.bfloat16)
        contrib = jnp.einsum(
            "sqm,smj->sqj",
            lefts,
            select_blocks(right_table, right_now),
            preferred_element_type=jnp.float32,
        )
        placer = (aux_now[:, None] == aux_ids[None, :]).astype(jnp.float32)
        return (total + jnp.einsum("sa,sqj->aqj", placer, contrib), None)

    total, unused = lax.scan(step, start, (pieces, auxes, lefts_at, rights_at))
    return total


def on_device(tiles, tile_row, tile_col, tile_aux, coeffs):
    peers = lax.axis_size("row")
    tile = tiles.shape[1]
    occupied = coeffs.shape[1]
    blk_dev = coeffs.shape[0] // tile
    naux = AUX
    first = lax.axis_index("row") * blk_dev
    rows = tile_row[:, 0]
    cols = tile_col[:, 0]
    per_peer = CAP * blk_dev
    packed, aux_out, row_out, col_out = pack_for(
        tiles, cols // blk_dev, tile_aux, rows, cols, peers, per_peer, naux
    )
    got, got_aux, got_row, got_col = (
        lax.all_to_all(packed, "row", split_axis=0, concat_axis=0, tiled=True),
        lax.all_to_all(aux_out, "row", split_axis=0, concat_axis=0, tiled=True),
        lax.all_to_all(row_out, "row", split_axis=0, concat_axis=0, tiled=True),
        lax.all_to_all(col_out, "row", split_axis=0, concat_axis=0, tiled=True),
    )
    batch_whole = lax.all_gather(coeffs[:, :OI], "row", axis=0, tiled=True)
    local_full = coeffs.reshape(blk_dev, tile, occupied)
    right_index = jnp.clip(got_col - first, 0, blk_dev - 1)
    total = contract(
        got, got_aux, got_row, right_index, batch_whole.reshape(-1, tile, OI), local_full, naux
    )
    return lax.psum_scatter(total, "row", scatter_dimension=2, tiled=True)


def solution(mesh):
    placed = (
        P(("groups", "row"), None, None),
        P(("groups", "row"), None),
        P(("groups", "row"), None),
        P(("groups", "row")),
        P(("groups", "row"), None),
    )
    return jax.shard_map(
        on_device, mesh=mesh, in_specs=placed, out_specs=P("groups", None, "row"), check_vma=False
    )
```

profile of v0, /device:TPU:0, one launch (start us, length us, event | category | flops | bytes accessed | tf_op | source)
XLA Modules:
  0.0 457.7 jit_solution(13943104675487700670)
XLA Ops:
  10.4 7.4 %all-to-all-start.1 = ((s32[16,8,1]{1,2,0:T(1,128)}), s32[16,8,1]{1,2,0:T(1,128)S(1)}, u32[]{:S(2)}, u32[]{:S(2)}) async-start(s32[16,8,1]{1,2,0:T(1,128)} %bitcast.6), calls=%async_computation.1 | async-start | bytes 16384 | tf_op jit(solution)/shard_map/all_to_all | solution.py:89
  18.5 5.6 %all-to-all-done.1 = s32[16,8,1]{1,2,0:T(1,128)S(1)} async-done(((s32[16,8,1]{1,2,0:T(1,128)}), s32[16,8,1]{1,2,0:T(1,128)S(1)}, u32[]{:S(2)}, u32[]{:S(2)}) %all-to-all-start.1) | async-done | bytes 544 | tf_op jit(solution)/shard_map/all_to_all | solution.py:89
  24.2 3.5 all-to-all-start
  28.3 5.6 %all-to-all-done = s32[16,8,1]{1,2,0:T(1,128)S(1)} async-done(((s32[16,8,1]{1,2,0:T(1,128)}), s32[16,8,1]{1,2,0:T(1,128)S(1)}, u32[]{:S(2)}, u32[]{:S(2)}) %all-to-all-start) | async-done | bytes 544 | tf_op jit(solution)/shard_map/all_to_all | solution.py:88
  33.9 3.5 all-to-all-start.3
  37.4 2.0 convolution_convert_fusion.3
  39.5 4.7 %copy.40 = bf16[128,128,128]{2,1,0:T(8,128)(2,1)} copy(bf16[128,128,128]{2,0,1:T(8,128)(2,1)S(1)} %convolution_convert_fusion.3) | data formatting | bytes 8388608 | tf_op jit(solution)/shard_map/convert_element_type | solution.py:22
  44.2 6.0 %all-to-all-start.2 = ((bf16[128,128,128]{2,1,0:T(8,128)(2,1)}), bf16[128,128,128]{2,1,0:T(8,128)(2,1)}, u32[]{:S(2)}, u32[]{:S(2)}) async-start(bf16[128,128,128]{2,1,0:T(8,128)(2,1)} %copy.40), calls=%async_computation.2 | async-start | bytes 8388608 | tf_op jit(solution)/shard_map/all_to_all | solution.py:87
  50.2 1.6 slice.3
  52.1 2.0 copy.42
  56.1 79.2 %all-gather.2.cloned.1.call-done = bf16[8192,96]{1,0:T(8,128)(2,1)} async-done(((bf16[512,96]{1,0:T(8,128)(2,1)}), bf16[8192,96]{1,0:T(8,128)(2,1)}) %all-gather.2.cloned.1.call-update) | async-done | bytes 1572880 | tf_op jit(solution)/shard_map/all_gather | solution.py:92
  135.3 3.9 copy.44
  139.2 1.3 all-to-all-done.2
  140.5 182.1 %while.11 = (s32[]{:T(128)}, f32[16,96,1024]{2,0,1:T(8,128)}, s32[8,16]{1,0:T(8,128)S(1)}, s32[8,16]{1,0:T(8,128)S(1)}, bf16[64,128,96]{1,0,2:T(8,128)(2,1)}, /*...) while((s32[]{:T(128)}, f32[16,96,1024]{2,0,1:T(8,128)}, ...), condition=%wide.region_6.7_spmd.clone, body=%wide.region_5.6_spmd.clone.sunk | while | flops 550896960 | bytes 31195844 | solution.py:69
  140.5 1.8 convolution_convert_fusion.7
  142.3 3.0 convolution_convert_fusion.6
  145.4 9.2 %fusion.61 = bf16[16,96,1024]{2,1,0:T(8,128)(2,1)} fusion(bf16[16,128,1024]{2,0,1:T(8,128)(2,1)} %convolution_convert_fusion.6, bf16[8,16,128,128]{3,2,1,0:T(8,128)(2,1)} %get-tuple-element.213, s32[]{:T(128)S(6)} %copy.64, bf16[16,128,96]{1,0,2:T(8,128)(2,1)S(1)} %convolution_convert_fusion.7), kind=kOutput, calls=%fused_computation.4.clone.1 | convolution fusion | flops 453181440 | bytes 8257540 | tf_op jit(solution)/shard_map/while/body/eval_jaxpr/sqm,smj->sqj/dot_general | solution.py:60
  154.6 7.0 %select_add_fusion.2 = f32[16,96,1024]{2,0,1:T(8,128)} fusion(f32[16,96,1024]{2,0,1:T(8,128)} %get-tuple-element.199, pred[]{:T(512)S(6)} %compare.14, bf16[16,96,1024]{2,1,0:T(8,128)(2,1)} %fusion.61, s32[16]{0:T(128)S(1)} %get-tuple-element.187), kind=kOutput, calls=%fused_computation.3.clone.1 | convolution fusion | flops 53477632 | bytes 15728705 | tf_op jit(solution)/shard_map/while/body/eval_jaxpr/sa,sqj->aqj/dot_general | solution.py:67
  161.7 1.8 convolution_convert_fusion.7
  163.5 3.0 convolution_convert_fusion.6
  166.5 9.2 %fusion.61 = bf16[16,96,1024]{2,1,0:T(8,128)(2,1)} fusion(bf16[16,128,1024]{2,0,1:T(8,128)(2,1)} %convolution_convert_fusion.6, bf16[8,16,128,128]{3,2,1,0:T(8,128)(2,1)} %get-tuple-element.213, s32[]{:T(128)S(6)} %copy.64, bf16[16,128,96]{1,0,2:T(8,128)(2,1)S(1)} %convolution_convert_fusion.7), kind=kOutput, calls=%fused_computation.4.clone.1 | convolution fusion | flops 453181440 | bytes 8257540 | tf_op jit(solution)/shard_map/while/body/eval_jaxpr/sqm,smj->sqj/dot_general | solution.py:60
  175.8 8.9 %select_add_fusion.2 = f32[16,96,1024]{2,0,1:T(8,128)} fusion(f32[16,96,1024]{2,0,1:T(8,128)} %get-tuple-element.199, pred[]{:T(512)S(6)} %compare.14, bf16[16,96,1024]{2,1,0:T(8,128)(2,1)} %fusion.61, s32[16]{0:T(128)S(1)} %get-tuple-element.187), kind=kOutput, calls=%fused_computation.3.clone.1 | convolution fusion | flops 53477632 | bytes 15728705 | tf_op jit(solution)/shard_map/while/body/eval_jaxpr/sa,sqj->aqj/dot_general | solution.py:67
  184.7 1.8 convolution_convert_fusion.7
  186.5 3.0 convolution_convert_fusion.6
  189.5 9.2 %fusion.61 = bf16[16,96,1024]{2,1,0:T(8,128)(2,1)} fusion(bf16[16,128,1024]{2,0,1:T(8,128)(2,1)} %convolution_convert_fusion.6, bf16[8,16,128,128]{3,2,1,0:T(8,128)(2,1)} %get-tuple-element.213, s32[]{:T(128)S(6)} %copy.64, bf16[16,128,96]{1,0,2:T(8,128)(2,1)S(1)} %convolution_convert_fusion.7), kind=kOutput, calls=%fused_computation.4.clone.1 | convolution fusion | flops 453181440 | bytes 8257540 | tf_op jit(solution)/shard_map/while/body/eval_jaxpr/sqm,smj->sqj/dot_general | solution.py:60
  198.8 8.9 %select_add_fusion.2 = f32[16,96,1024]{2,0,1:T(8,128)} fusion(f32[16,96,1024]{2,0,1:T(8,128)} %get-tuple-element.199, pred[]{:T(512)S(6)} %compare.14, bf16[16,96,1024]{2,1,0:T(8,128)(2,1)} %fusion.61, s32[16]{0:T(128)S(1)} %get-tuple-element.187), kind=kOutput, calls=%fused_computation.3.clone.1 | convolution fusion | flops 53477632 | bytes 15728705 | tf_op jit(solution)/shard_map/while/body/eval_jaxpr/sa,sqj->aqj/dot_general | solution.py:67
  207.7 1.8 convolution_convert_fusion.7
  209.5 3.0 convolution_convert_fusion.6
  212.5 9.2 %fusion.61 = bf16[16,96,1024]{2,1,0:T(8,128)(2,1)} fusion(bf16[16,128,1024]{2,0,1:T(8,128)(2,1)} %convolution_convert_fusion.6, bf16[8,16,128,128]{3,2,1,0:T(8,128)(2,1)} %get-tuple-element.213, s32[]{:T(128)S(6)} %copy.64, bf16[16,128,96]{1,0,2:T(8,128)(2,1)S(1)} %convolution_convert_fusion.7), kind=kOutput, calls=%fused_computation.4.clone.1 | convolution fusion | flops 453181440 | bytes 8257540 | tf_op jit(solution)/shard_map/while/body/eval_jaxpr/sqm,smj->sqj/dot_general | solution.py:60
  221.7 8.9 %select_add_fusion.2 = f32[16,96,1024]{2,0,1:T(8,128)} fusion(f32[16,96,1024]{2,0,1:T(8,128)} %get-tuple-element.199, pred[]{:T(512)S(6)} %compare.14, bf16[16,96,1024]{2,1,0:T(8,128)(2,1)} %fusion.61, s32[16]{0:T(128)S(1)} %get-tuple-element.187), kind=kOutput, calls=%fused_computation.3.clone.1 | convolution fusion | flops 53477632 | bytes 15728705 | tf_op jit(solution)/shard_map/while/body/eval_jaxpr/sa,sqj->aqj/dot_general | solution.py:67
  230.7 1.8 convolution_convert_fusion.7
  232.5 3.0 convolution_convert_fusion.6
  235.5 9.2 %fusion.61 = bf16[16,96,1024]{2,1,0:T(8,128)(2,1)} fusion(bf16[16,128,1024]{2,0,1:T(8,128)(2,1)} %convolution_convert_fusion.6, bf16[8,16,128,128]{3,2,1,0:T(8,128)(2,1)} %get-tuple-element.213, s32[]{:T(128)S(6)} %copy.64, bf16[16,128,96]{1,0,2:T(8,128)(2,1)S(1)} %convolution_convert_fusion.7), kind=kOutput, calls=%fused_computation.4.clone.1 | convolution fusion | flops 453181440 | bytes 8257540 | tf_op jit(solution)/shard_map/while/body/eval_jaxpr/sqm,smj->sqj/dot_general | solution.py:60
  244.7 8.9 %select_add_fusion.2 = f32[16,96,1024]{2,0,1:T(8,128)} fusion(f32[16,96,1024]{2,0,1:T(8,128)} %get-tuple-element.199, pred[]{:T(512)S(6)} %compare.14, bf16[16,96,1024]{2,1,0:T(8,128)(2,1)} %fusion.61, s32[16]{0:T(128)S(1)} %get-tuple-element.187), kind=kOutput, calls=%fused_computation.3.clone.1 | convolution fusion | flops 53477632 | bytes 15728705 | tf_op jit(solution)/shard_map/while/body/eval_jaxpr/sa,sqj->aqj/dot_general | solution.py:67
  253.7 1.8 convolution_convert_fusion.7
  255.5 3.0 convolution_convert_fusion.6
  258.5 9.2 %fusion.61 = bf16[16,96,1024]{2,1,0:T(8,128)(2,1)} fusion(bf16[16,128,1024]{2,0,1:T(8,128)(2,1)} %convolution_convert_fusion.6, bf16[8,16,128,128]{3,2,1,0:T(8,128)(2,1)} %get-tuple-element.213, s32[]{:T(128)S(6)} %copy.64, bf16[16,128,96]{1,0,2:T(8,128)(2,1)S(1)} %convolution_convert_fusion.7), kind=kOutput, calls=%fused_computation.4.clone.1 | convolution fusion | flops 453181440 | bytes 8257540 | tf_op jit(solution)/shard_map/while/body/eval_jaxpr/sqm,smj->sqj/dot_general | solution.py:60
  267.7 8.9 %select_add_fusion.2 = f32[16,96,1024]{2,0,1:T(8,128)} fusion(f32[16,96,1024]{2,0,1:T(8,128)} %get-tuple-element.199, pred[]{:T(512)S(6)} %compare.14, bf16[16,96,1024]{2,1,0:T(8,128)(2,1)} %fusion.61, s32[16]{0:T(128)S(1)} %get-tuple-element.187), kind=kOutput, calls=%fused_computation.3.clone.1 | convolution fusion | flops 53477632 | bytes 15728705 | tf_op jit(solution)/shard_map/while/body/eval_jaxpr/sa,sqj->aqj/dot_general | solution.py:67
  276.7 1.8 convolution_convert_fusion.7
  278.4 3.0 convolution_convert_fusion.6
  281.5 9.2 %fusion.61 = bf16[16,96,1024]{2,1,0:T(8,128)(2,1)} fusion(bf16[16,128,1024]{2,0,1:T(8,128)(2,1)} %convolution_convert_fusion.6, bf16[8,16,128,128]{3,2,1,0:T(8,128)(2,1)} %get-tuple-element.213, s32[]{:T(128)S(6)} %copy.64, bf16[16,128,96]{1,0,2:T(8,128)(2,1)S(1)} %convolution_convert_fusion.7), kind=kOutput, calls=%fused_computation.4.clone.1 | convolution fusion | flops 453181440 | bytes 8257540 | tf_op jit(solution)/shard_map/while/body/eval_jaxpr/sqm,smj->sqj/dot_general | solution.py:60
  290.7 8.9 %select_add_fusion.2 = f32[16,96,1024]{2,0,1:T(8,128)} fusion(f32[16,96,1024]{2,0,1:T(8,128)} %get-tuple-element.199, pred[]{:T(512)S(6)} %compare.14, bf16[16,96,1024]{2,1,0:T(8,128)(2,1)} %fusion.61, s32[16]{0:T(128)S(1)} %get-tuple-element.187), kind=kOutput, calls=%fused_computation.3.clone.1 | convolution fusion | flops 53477632 | bytes 15728705 | tf_op jit(solution)/shard_map/while/body/eval_jaxpr/sa,sqj->aqj/dot_general | solution.py:67
  299.6 1.8 convolution_convert_fusion.7
  301.4 3.0 convolution_convert_fusion.6
  304.5 9.2 %fusion.61 = bf16[16,96,1024]{2,1,0:T(8,128)(2,1)} fusion(bf16[16,128,1024]{2,0,1:T(8,128)(2,1)} %convolution_convert_fusion.6, bf16[8,16,128,128]{3,2,1,0:T(8,128)(2,1)} %get-tuple-element.213, s32[]{:T(128)S(6)} %copy.64, bf16[16,128,96]{1,0,2:T(8,128)(2,1)S(1)} %convolution_convert_fusion.7), kind=kOutput, calls=%fused_computation.4.clone.1 | convolution fusion | flops 453181440 | bytes 8257540 | tf_op jit(solution)/shard_map/while/body/eval_jaxpr/sqm,smj->sqj/dot_general | solution.py:60
  313.7 8.9 %select_add_fusion.2 = f32[16,96,1024]{2,0,1:T(8,128)} fusion(f32[16,96,1024]{2,0,1:T(8,128)} %get-tuple-element.199, pred[]{:T(512)S(6)} %compare.14, bf16[16,96,1024]{2,1,0:T(8,128)(2,1)} %fusion.61, s32[16]{0:T(128)S(1)} %get-tuple-element.187), kind=kOutput, calls=%fused_computation.3.clone.1 | convolution fusion | flops 53477632 | bytes 15728705 | tf_op jit(solution)/shard_map/while/body/eval_jaxpr/sa,sqj->aqj/dot_general | solution.py:67
  322.6 8.2 %copy.43 = f32[16,96,1024]{1,2,0:T(8,128)} copy(f32[16,96,1024]{2,0,1:T(8,128)} %get-tuple-element.52) | data formatting | bytes 12582912 | tf_op jit(solution)/shard_map/while | solution.py:69
  330.9 120.0 %reduce-scatter.2.cloned.1.call-done = f32[16,96,64]{1,2,0:T(8,128)} async-done(((f32[16,96,1024]{1,2,0:T(8,128)}), f32[16,96,64]{1,2,0:T(8,128)}) %reduce-scatter.2.cloned.1.call-update) | async-done | bytes 393232 | tf_op jit(solution)/shard_map/reduce_scatter | solution.py:98
  (41 shorter events, 7.6 us)
Async XLA Ops:
  6.5 30.9 %copy-start = (bf16[64,128,128]{2,1,0:T(8,128)(2,1)S(1)}, bf16[64,128,128]{2,1,0:T(8,128)(2,1)}, u32[]{:S(2)}) copy-start(bf16[64,128,128]{2,1,0:T(8,128)(2,1)} %param.7) | copy-start | bytes 6291460
  10.4 13.8 %all-to-all-start.1 = ((s32[16,8,1]{1,2,0:T(1,128)}), s32[16,8,1]{1,2,0:T(1,128)S(1)}, u32[]{:S(2)}, u32[]{:S(2)}) async-start(s32[16,8,1]{1,2,0:T(1,128)} %bitcast.6), calls=%async_computation.1 | async-start | bytes 16384 | tf_op jit(solution)/shard_map/all_to_all | solution.py:89
  24.2 9.8 %all-to-all-start = ((s32[16,8,1]{1,2,0:T(1,128)}), s32[16,8,1]{1,2,0:T(1,128)S(1)}, u32[]{:S(2)}, u32[]{:S(2)}) async-start(s32[16,8,1]{1,2,0:T(1,128)} %bitcast.4), calls=%async_computation | async-start | bytes 16384 | tf_op jit(solution)/shard_map/all_to_all | solution.py:88
  33.9 10.2 %all-to-all-start.3 = ((s32[16,8,1]{1,2,0:T(1,128)}), s32[16,8,1]{1,2,0:T(1,128)S(1)}, u32[]{:S(2)}, u32[]{:S(2)}) async-start(s32[16,8,1]{1,2,0:T(1,128)} %bitcast.10), calls=%async_computation.3 | async-start | bytes 16384 | tf_op jit(solution)/shard_map/all_to_all | solution.py:90
  44.2 96.3 %all-to-all-start.2 = ((bf16[128,128,128]{2,1,0:T(8,128)(2,1)}), bf16[128,128,128]{2,1,0:T(8,128)(2,1)}, u32[]{:S(2)}, u32[]{:S(2)}) async-start(bf16[128,128,128]{2,1,0:T(8,128)(2,1)} %copy.40), calls=%async_computation.2 | async-start | bytes 8388608 | tf_op jit(solution)/shard_map/all_to_all | solution.py:87
  50.2 85.1 %all-gather.2.cloned.1.call-start = ((), (), s32[]{:S(2)}) async-start(), calls=%async_computation.5 | async-start | bytes 2228224 | tf_op jit(solution)/shard_map/all_gather | solution.py:92
  51.8 399.0 %reduce-scatter.2.cloned.1.call-start = ((), (), s32[]{:S(2)}) async-start(), calls=%async_computation.6 | async-start | bytes 8912896 | tf_op jit(solution)/shard_map/reduce_scatter | solution.py:98
Sparse Core Ops, SparseCore 0:
  53.2 82.0 all-gather.1
  331.0 119.8 reduce-scatter.1
where the time goes:
time: 459 us; the launch traced here: 458 us
  waiting for transfers between devices  212 us (46%)
  matrix products  184 us (40%)
  local copies, waits for them, and re-layouts  23.3 us (5%)
  starting transfers between devices  20.6 us (4%)
  between operations  13.5 us (3%)
    reduce_scatter x1, waiting for transfers between devices, on_device(): return lax.psum_scatter(total, 'row', scatter_dimension=2, tiled=True)  120 us
    all_gather x1, waiting for transfers between devices, on_device(): batch_whole = lax.all_gather(coeffs[:, :OI], 'row', axis=0, tiled=True)  79.2 us
    dot_general x8, matrix products, step(): jnp.einsum('sqm,smj->sqj', lefts, select_blocks(right_table, right_now),...  73.9 us
    dot_general x8, matrix products, step(): return (total + jnp.einsum('sa,sqj->aqj', placer, contrib), None)  69.3 us
    dot_general x16, matrix products, select_blocks(): jnp.einsum('sb,bnj->snj', picker, table, preferred_element_type=jnp.float32)  38.7 us
  transfers between devices with their start and end apart: 6, of which 5 were waited for; matrix products, arithmetic and copies ran while one was open for 4% of the time, Pallas kernels for 0%

commit v1 on v0

v1 whole, which is shorter than its diff:
```python
import functools
import jax
import jax.numpy as jnp
from jax import lax
from jax.experimental import pallas as pl
from jax.experimental.pallas import tpu as pltpu
from jax.sharding import PartitionSpec as P

OI = 96
AUX = 16
CAP = 2
MESH = pl.DeviceIdType.MESH
VMEM = pl.BlockSpec(memory_space=pltpu.VMEM)
SMEM = pl.BlockSpec(memory_space=pltpu.SMEM)
ANY = pl.BlockSpec(memory_space=pl.ANY)
LIMIT = 48 * 1024 * 1024


def greet(peers):
    barrier = pltpu.get_barrier_semaphore()
    for peer in peers:
        pl.semaphore_signal(barrier, inc=1, device_id={"row": peer}, device_id_type=MESH)
    pl.semaphore_wait(barrier, len(peers))


def remote(src, dst, send, recv, peer):
    return pltpu.make_async_remote_copy(
        src_ref=src, dst_ref=dst, send_sem=send, recv_sem=recv,
        device_id={"row": peer}, device_id_type=MESH,
    )


def gather_kernel(devices, own_ref, all_ref, zs, zr, ys, yr, cs, cr):
    me = lax.axis_index("row")
    blk = own_ref.shape[0]
    depth = devices // 4
    z, y, core = me // 4, (me // 2) % 2, me % 2

    def index(zz, yy, cc):
        return (zz * 2 + yy) * 2 + cc

    def at(dev):
        return all_ref.at[pl.ds(dev * blk, blk)]

    z_peers = [index((z + i) % depth, y, core) for i in range(1, depth)]
    over_y, over_core = index(z, 1 - y, core), index(z, y, 1 - core)
    greet(z_peers + [over_y, over_core])
    all_ref[pl.ds(me * blk, blk)] = own_ref[...]
    copies = []
    z_copies = []
    for i, peer in enumerate(z_peers):
        copy = remote(own_ref, at(me), zs.at[i], zr.at[i], peer)
        copy.start()
        z_copies.append(copy)
    y_copies, c_copies = [], []

    def forward_y(i, dev):
        src = own_ref if i == 0 else at(dev)
        copy = remote(src, at(dev), ys.at[i], yr.at[i], over_y)
        copy.start()
        y_copies.append(copy)

    def forward_core(i, dev):
        src = own_ref if i == 0 else at(dev)
        copy = remote(src, at(dev), cs.at[i], cr.at[i], over_core)
        copy.start()
        c_copies.append(copy)

    forward_y(0, me)
    forward_core(0, me)
    for i in range(1, depth):
        z_copies[i - 1].wait_recv()
        dev = index((z + depth - i) % depth, y, core)
        forward_y(i, dev)
        forward_core(i, dev)
    for i in range(depth):
        y_copies[i].wait_recv()
        forward_core(depth + i, index((z + depth - i) % depth, 1 - y, core))
    for copy in c_copies:
        copy.wait_recv()
    for copy in z_copies + y_copies + c_copies:
        copy.wait_send()


def gather(own, devices):
    depth = devices // 4
    dma = pltpu.SemaphoreType.DMA
    return pl.pallas_call(
        functools.partial(gather_kernel, devices),
        out_shape=jax.ShapeDtypeStruct((devices * own.shape[0],) + own.shape[1:], own.dtype),
        in_specs=[VMEM],
        out_specs=VMEM,
        scratch_shapes=[dma((depth,))] * 4 + [dma((2 * depth,))] * 2,
        compiler_params=pltpu.CompilerParams(
            collective_id=0, has_side_effects=True, vmem_limit_bytes=LIMIT
        ),
    )(own)


def left_kernel(row_ref, col_ref, aux_ref, batch_ref, tiles_ref, packed_ref, marks_ref, seen_ref):
    count = tiles_ref.shape[0]
    slots = marks_ref.shape[0]
    marks_ref[...] = jnp.full(marks_ref.shape, AUX, jnp.int32)

    def clear(b, carry):
        seen_ref[b] = 0
        return carry

    lax.fori_loop(0, slots // CAP, clear, 0)
    width = 8

    def step(g, carry):
        lefts = []
        for u in range(width):
            t = g * width + u
            lefts.append(
                jnp.dot(
                    batch_ref[row_ref[t, 0]], tiles_ref[t], preferred_element_type=jnp.float32
                ).astype(jnp.bfloat16)
            )
        for u in range(width):
            t = g * width + u
            c = col_ref[t, 0]
            rank = seen_ref[c]
            seen_ref[c] = rank + 1
            slot = c * CAP + rank
            packed_ref[slot] = lefts[u]
            marks_ref[slot] = jnp.full((1, 128), aux_ref[t], jnp.int32)
        return carry

    lax.fori_loop(0, count // width, step, 0)


def lefts(tile_row, tile_col, tile_aux, batch, tiles):
    slots = batch.shape[0] * CAP
    tile = tiles.shape[1]
    return pl.pallas_call(
        left_kernel,
        out_shape=[
            jax.ShapeDtypeStruct((slots, OI, tile), jnp.bfloat16),
            jax.ShapeDtypeStruct((slots, 1, 128), jnp.int32),
        ],
        in_specs=[SMEM, SMEM, SMEM, VMEM, VMEM],
        out_specs=[VMEM, VMEM],
        scratch_shapes=[pltpu.SMEM((batch.shape[0],), jnp.int32)],
        compiler_params=pltpu.CompilerParams(vmem_limit_bytes=LIMIT),
    )(tile_row, tile_col, tile_aux, batch, tiles)


def exchange_kernel(devices, x_ref, m_ref, x_out, m_out, own, xs, xr, ms, mr):
    me = lax.axis_index("row")
    per = x_ref.shape[0] // devices

    def part(ref, dev):
        return ref.at[pl.ds(dev * per, per)]

    peers = [(me + i) % devices for i in range(1, devices)]
    greet(peers)
    copies = []
    for i, peer in enumerate(peers):
        copies.append(remote(part(m_ref, peer), part(m_out, me), ms.at[i], mr.at[i], peer))
        copies.append(remote(part(x_ref, peer), part(x_out, me), xs.at[i], xr.at[i], peer))
    for copy in copies:
        copy.start()
    mine = [
        pltpu.make_async_copy(part(x_ref, me), part(x_out, me), own.at[0]),
        pltpu.make_async_copy(part(m_ref, me), part(m_out, me), own.at[1]),
    ]
    for copy in mine:
        copy.start()
    for copy in mine:
        copy.wait()
    for copy in copies:
        copy.wait_recv()
    for copy in copies:
        copy.wait_send()


def exchange(x, marks, devices):
    dma = pltpu.SemaphoreType.DMA
    return pl.pallas_call(
        functools.partial(exchange_kernel, devices),
        out_shape=[
            jax.ShapeDtypeStruct(x.shape, x.dtype),
            jax.ShapeDtypeStruct(marks.shape, marks.dtype),
        ],
        in_specs=[ANY, ANY],
        out_specs=[ANY, ANY],
        scratch_shapes=[dma((2,))] + [dma((devices,))] * 4,
        compiler_params=pltpu.CompilerParams(collective_id=1, has_side_effects=True),
    )(x, marks)


def place_kernel(devices, aux_ref, got_ref, coeffs_ref, out_ref, sums, dense):
    blk = sums.shape[0]
    sums[...] = jnp.zeros_like(sums)

    def add(p, carry):
        for b in range(blk):
            for r in range(CAP):
                s = (p * blk + b) * CAP + r
                a = aux_ref[s]
                sums[b, a] += got_ref[s].astype(jnp.float32)
        return carry

    lax.fori_loop(0, devices, add, 0)
    tile = got_ref.shape[2]
    for b in range(blk):
        for a in range(AUX):
            dense[pl.ds(a * OI, OI), pl.ds(b * tile, tile)] = sums[b, a].astype(jnp.bfloat16)
    width = out_ref.shape[2]
    chips = devices // 2

    def column(n, carry):
        turned = coeffs_ref[n]
        whole = lax.dot_general(
            turned, dense[...], (((1,), (1,)), ((), ())), preferred_element_type=jnp.float32
        ).astype(jnp.bfloat16)
        out_ref[0, n] = whole[:width]
        out_ref[1, n] = whole[width:]
        return carry

    lax.fori_loop(0, chips, column, 0)


def place(aux, got, turned, devices):
    chips, both, depth = turned.shape
    tile = got.shape[2]
    return pl.pallas_call(
        functools.partial(place_kernel, devices),
        out_shape=jax.ShapeDtypeStruct((2, chips, both // 2, AUX * OI), jnp.bfloat16),
        in_specs=[SMEM, VMEM, VMEM],
        out_specs=VMEM,
        scratch_shapes=[
            pltpu.VMEM((depth // tile, AUX + 1, OI, tile), jnp.float32),
            pltpu.VMEM((AUX * OI, depth), jnp.bfloat16),
        ],
        compiler_params=pltpu.CompilerParams(vmem_limit_bytes=LIMIT),
    )(aux, got, turned)


def reduce_kernel(devices, part_ref, out_ref, near, held, far, a_s, a_r, b_s, b_r):
    me = lax.axis_index("row")
    chips = devices // 2
    chip, core = me // 2, me % 2
    partner = chip * 2 + 1 - core
    peers = [((chip + i) % chips) * 2 + core for i in range(1, chips)]
    greet(peers + [partner])
    first = []
    for i in range(1, chips + 1):
        n = (chip + i) % chips
        copy = remote(part_ref.at[1 - core, n], near.at[n], a_s.at[i - 1], a_r.at[i - 1], partner)
        copy.start()
        first.append(copy)
    second = []
    for i in range(1, chips):
        n = (chip + i) % chips
        first[i - 1].wait_recv()
        held[n] = (
            part_ref[core, n].astype(jnp.float32) + near[n].astype(jnp.float32)
        ).astype(jnp.bfloat16)
        copy = remote(held.at[n], far.at[chip], b_s.at[i - 1], b_r.at[i - 1], peers[i - 1])
        copy.start()
        second.append(copy)
    first[chips - 1].wait_recv()
    out_ref[...] = part_ref[core, chip].astype(jnp.float32) + near[chip].astype(jnp.float32)
    for i in range(1, chips):
        second[i - 1].wait_recv()
        out_ref[...] += far[(chip + chips - i) % chips].astype(jnp.float32)
    for copy in first + second:
        copy.wait_send()


def reduce(part, devices):
    chips = devices // 2
    block = part.shape[2:]
    dma = pltpu.SemaphoreType.DMA
    slots = pltpu.VMEM((chips,) + block, jnp.bfloat16)
    return pl.pallas_call(
        functools.partial(reduce_kernel, devices),
        out_shape=jax.ShapeDtypeStruct(block, jnp.float32),
        in_specs=[VMEM],
        out_specs=VMEM,
        scratch_shapes=[slots] * 3 + [dma((chips,))] * 4,
        compiler_params=pltpu.CompilerParams(
            collective_id=2, has_side_effects=True, vmem_limit_bytes=LIMIT
        ),
    )(part)


def on_device(devices, tiles, tile_row, tile_col, tile_aux, coeffs):
    tile = tiles.shape[1]
    rows, occupied = coeffs.shape
    chips = devices // 2
    own = coeffs[:, :OI].reshape(rows // tile, tile, OI).transpose(0, 2, 1)
    turned = coeffs.T.reshape(chips, occupied // chips, rows)
    batch = gather(own, devices)
    packed, marks = lefts(tile_row, tile_col, tile_aux, batch, tiles)
    got, got_marks = exchange(packed, marks, devices)
    part = place(got_marks[:, 0, 0], got, turned, devices)
    total = reduce(part, devices)
    return total.T.reshape(AUX, OI, occupied // devices)


def solution(mesh):
    placed = (
        P(("groups", "row"), None, None),
        P(("groups", "row"), None),
        P(("groups", "row"), None),
        P(("groups", "row")),
        P(("groups", "row"), None),
    )
    return jax.shard_map(
        functools.partial(on_device, mesh.shape["row"]),
        mesh=mesh, in_specs=placed, out_specs=P("groups", None, "row"), check_vma=False,
    )
```

time: 459 us -> 156 us (0.34)
  the two profiles are of different devices: /device:TPU:0 before, /device:TPU:14 now
where the time goes in v1:
time: 156 us
  Pallas kernels  145 us (93%)
  local copies, waits for them, and re-layouts  10.4 us (7%)
    pallas_call x1, Pallas kernels, exchange(): pl.pallas_call(functools.partial(exchange_kernel, devices), out_shape=[ja...  75 us
    pallas_call x1, Pallas kernels, reduce(): pl.pallas_call(functools.partial(reduce_kernel, devices), out_shape=jax.S...  40.3 us
    pallas_call x1, Pallas kernels, gather(): pl.pallas_call(functools.partial(gather_kernel, devices), out_shape=jax.S...  16.4 us
    pallas_call x1, Pallas kernels, place(): pl.pallas_call(functools.partial(place_kernel, devices), out_shape=jax.Sh...  8.26 us
    pallas_call x1, Pallas kernels, lefts(): pl.pallas_call(left_kernel, out_shape=[jax.ShapeDtypeStruct((slots, OI, t...  5.45 us
    unnamed x10, local copies, waits for them, and re-layouts  4.37 us
    slice x1, local copies, waits for them, and re-layouts, on_device(): part = place(got_marks[:, 0, 0], got, turned, devices)  3.28 us

profile of v1, /device:TPU:14, one launch (start us, length us, event | category | flops | bytes accessed | tf_op | source)
XLA Modules:
  0.0 155.8 jit_solution(7791368054659821265)
XLA Ops:
  0.0 0.9 slice.6
  0.9 0.1 copy.11
  1.0 16.4 %shard_map.55.batch_ref = bf16[64,96,128]{2,1,0:T(8,128)(2,1)S(1)} custom-call(bf16[4,96,128]{2,1,0:T(8,128)(2,1)S(1)} %bitcast.9), custom_call_target="tpu_custom_call" | custom-call | tf_op jit(solution)/shard_map/pallas_call | solution.py:88
  17.5 0.7 copy.12.row_ref
  18.2 0.7 copy.13.col_ref
  19.0 0.0 copy-start
  19.0 1.6 %copy-done = bf16[64,128,128]{2,1,0:T(8,128)(2,1)S(1)} copy-done((bf16[64,128,128]{2,1,0:T(8,128)(2,1)S(1)}, bf16[64,128,128]{2,1,0:T(8,128)(2,1)}, u32[]{:S(2)}) %copy-start) | copy-done | bytes 2097176
  20.6 0.0 copy-start.2
  20.6 0.7 copy-done.2
  21.2 0.0 copy-start.3
  21.2 5.4 %shard_map.56 = (bf16[128,96,128]{2,1,0:T(8,128)(2,1)}, s32[128,1,128]{2,1,0:T(1,128)S(1)}) custom-call(s32[64,1]{1,0:T(8,128)S(1)} %copy.12.row_ref, s32[64,1]{1,0:T(8,128)S(1)} %copy.13.col_ref, s32[64]{0:T(128)S(1)} %copy-done.2, bf16[64,96,128]{2,1,0:T(8,128)(2,1)S(1)} %shard_map.55.batch_ref, bf16[64,128,128]{2,1,0:T(8,128)(2,1)S(1)} %copy-done), custom_call_target="tpu_custom_call" | custom-call | tf_op jit(solution)/shard_map/pallas_call | solution.py:137
  26.7 0.0 copy-start.1
  26.7 0.6 copy-done.1
  27.3 75.0 %shard_map.57 = (bf16[128,96,128]{2,1,0:T(8,128)(2,1)}, s32[128,1,128]{2,1,0:T(1,128)}) custom-call(bf16[128,96,128]{2,1,0:T(8,128)(2,1)} %get-tuple-element.9.x_ref, s32[128,1,128]{2,1,0:T(1,128)} %copy-done.1), custom_call_target="tpu_custom_call" | custom-call | tf_op jit(solution)/shard_map/pallas_call | solution.py:181
  102.3 3.3 %slice_reduce_fusion.aux_ref = s32[128]{0:T(128)S(1)} fusion(s32[128,1,128]{2,1,0:T(1,128)} %get-tuple-element.11), kind=kLoop, calls=%fused_computation | loop fusion | bytes 1024 | tf_op jit(solution)/shard_map/slice | solution.py:300
  105.6 0.0 copy-done.3
  105.6 0.5 copy.14
  106.1 8.3 %shard_map.58.part_ref = bf16[2,8,64,1536]{3,2,1,0:T(8,128)(2,1)S(1)} custom-call(s32[128]{0:T(128)S(1)} %slice_reduce_fusion.aux_ref, bf16[128,96,128]{2,1,0:T(8,128)(2,1)} %get-tuple-element.12.got_ref, bf16[8,128,512]{2,1,0:T(8,128)(2,1)S(1)} %bitcast.7), custom_call_target="tpu_custom_call" | custom-call | tf_op jit(solution)/shard_map/pallas_call | solution.py:229
  114.4 40.3 %shard_map.59 = f32[64,1536]{1,0:T(8,128)S(1)} custom-call(bf16[2,8,64,1536]{3,2,1,0:T(8,128)(2,1)S(1)} %shard_map.58.part_ref), custom_call_target="tpu_custom_call" | custom-call | tf_op jit(solution)/shard_map/pallas_call | solution.py:279
  154.7 0.2 reshape.11
  154.9 1.0 copy.15
Async XLA Ops:
  19.0 1.6 %copy-start = (bf16[64,128,128]{2,1,0:T(8,128)(2,1)S(1)}, bf16[64,128,128]{2,1,0:T(8,128)(2,1)}, u32[]{:S(2)}) copy-start(bf16[64,128,128]{2,1,0:T(8,128)(2,1)} %tiles_ref.1) | copy-start | bytes 6291460
  20.6 0.7 copy-start.2
  21.2 84.4 %copy-start.3 = (bf16[512,1024]{1,0:T(8,128)(2,1)S(1)}, bf16[512,1024]{1,0:T(8,128)(2,1)}, u32[]{:S(2)}) copy-start(bf16[512,1024]{1,0:T(8,128)(2,1)} %param.9) | copy-start | bytes 3145732
  26.7 0.6 copy-start.1

commit v2 on v1

v2 whole, which is shorter than its diff:
```python
import functools
import jax
import jax.numpy as jnp
from jax import lax
from jax.experimental import pallas as pl
from jax.experimental.pallas import tpu as pltpu
from jax.sharding import PartitionSpec as P

OI = 96
AUX = 16
CAP = 2
MESH = pl.DeviceIdType.MESH
VMEM = pl.BlockSpec(memory_space=pltpu.VMEM)
SMEM = pl.BlockSpec(memory_space=pltpu.SMEM)
ANY = pl.BlockSpec(memory_space=pl.ANY)
LIMIT = 48 * 1024 * 1024


def greet(peers):
    barrier = pltpu.get_barrier_semaphore()
    for peer in peers:
        pl.semaphore_signal(barrier, inc=1, device_id={"row": peer}, device_id_type=MESH)
    pl.semaphore_wait(barrier, len(peers))


def remote(src, dst, send, recv, peer):
    return pltpu.make_async_remote_copy(
        src_ref=src, dst_ref=dst, send_sem=send, recv_sem=recv,
        device_id={"row": peer}, device_id_type=MESH,
    )


def gather_kernel(devices, own_ref, all_ref, zs, zr, ys, yr, cs, cr):
    me = lax.axis_index("row")
    blk = own_ref.shape[0]
    depth = devices // 4
    z, y, core = me // 4, (me // 2) % 2, me % 2

    def index(zz, yy, cc):
        return (zz * 2 + yy) * 2 + cc

    def at(dev):
        return all_ref.at[pl.ds(dev * blk, blk)]

    z_peers = [index((z + i) % depth, y, core) for i in range(1, depth)]
    over_y, over_core = index(z, 1 - y, core), index(z, y, 1 - core)
    greet(z_peers + [over_y, over_core])
    all_ref[pl.ds(me * blk, blk)] = own_ref[...]
    copies = []
    z_copies = []
    for i, peer in enumerate(z_peers):
        copy = remote(own_ref, at(me), zs.at[i], zr.at[i], peer)
        copy.start()
        z_copies.append(copy)
    y_copies, c_copies = [], []

    def forward_y(i, dev):
        src = own_ref if i == 0 else at(dev)
        copy = remote(src, at(dev), ys.at[i], yr.at[i], over_y)
        copy.start()
        y_copies.append(copy)

    def forward_core(i, dev):
        src = own_ref if i == 0 else at(dev)
        copy = remote(src, at(dev), cs.at[i], cr.at[i], over_core)
        copy.start()
        c_copies.append(copy)

    forward_y(0, me)
    forward_core(0, me)
    for i in range(1, depth):
        z_copies[i - 1].wait_recv()
        dev = index((z + depth - i) % depth, y, core)
        forward_y(i, dev)
        forward_core(i, dev)
    for i in range(depth):
        y_copies[i].wait_recv()
        forward_core(depth + i, index((z + depth - i) % depth, 1 - y, core))
    for copy in c_copies:
        copy.wait_recv()
    for copy in z_copies + y_copies + c_copies:
        copy.wait_send()


def gather(own, devices):
    depth = devices // 4
    dma = pltpu.SemaphoreType.DMA
    return pl.pallas_call(
        functools.partial(gather_kernel, devices),
        out_shape=jax.ShapeDtypeStruct((devices * own.shape[0],) + own.shape[1:], own.dtype),
        in_specs=[VMEM],
        out_specs=VMEM,
        scratch_shapes=[dma((depth,))] * 4 + [dma((2 * depth,))] * 2,
        compiler_params=pltpu.CompilerParams(
            collective_id=0, has_side_effects=True, vmem_limit_bytes=LIMIT
        ),
    )(own)


def left_kernel(devices, row_ref, col_ref, aux_ref, batch_ref, tiles_ref, packed_ref, marks_ref, seen_ref):
    count = tiles_ref.shape[0]
    blocks = batch_ref.shape[0]
    half = devices // 2
    blk = blocks // devices
    per = 2 * blk * CAP

    def clear(b, carry):
        seen_ref[b] = 0
        for r in range(CAP):
            s = b * CAP + r
            marks_ref[lax.div(s, per), 0, lax.rem(s, per)] = AUX
        return carry

    lax.fori_loop(0, blocks, clear, 0)
    width = 8

    def step(g, carry):
        lefts = []
        for u in range(width):
            t = g * width + u
            lefts.append(
                jnp.dot(
                    batch_ref[row_ref[t, 0]], tiles_ref[t], preferred_element_type=jnp.float32
                ).astype(jnp.bfloat16)
            )
        for u in range(width):
            t = g * width + u
            c = col_ref[t, 0]
            rank = seen_ref[c]
            seen_ref[c] = rank + 1
            dev = lax.div(c, blk)
            dest = lax.rem(dev, half)
            at = (lax.div(dev, half) * blk + lax.rem(c, blk)) * CAP + rank
            packed_ref[dest * per + at] = lefts[u]
            marks_ref[dest, 0, at] = aux_ref[t]
        return carry

    lax.fori_loop(0, count // width, step, 0)


def lefts(tile_row, tile_col, tile_aux, batch, tiles, devices):
    slots = batch.shape[0] * CAP
    tile = tiles.shape[1]
    return pl.pallas_call(
        functools.partial(left_kernel, devices),
        out_shape=[
            jax.ShapeDtypeStruct((slots, OI, tile), jnp.bfloat16),
            jax.ShapeDtypeStruct((devices // 2, 1, 128), jnp.int32),
        ],
        in_specs=[SMEM, SMEM, SMEM, VMEM, VMEM],
        out_specs=[VMEM, SMEM],
        scratch_shapes=[pltpu.SMEM((batch.shape[0],), jnp.int32)],
        compiler_params=pltpu.CompilerParams(vmem_limit_bytes=LIMIT),
    )(tile_row, tile_col, tile_aux, batch, tiles)


def exchange_kernel(devices, x_ref, m_ref, x_out, m_out, own, xs, xr, ms, mr):
    me = lax.axis_index("row")
    half = devices // 2
    base, place_at = (me // half) * half, me % half
    per = x_ref.shape[0] // half

    def part(ref, j):
        return ref.at[pl.ds(j * per, per)]

    others = [(place_at + i) % half for i in range(1, half)]
    greet([base + j for j in others])
    copies = []
    for i, j in enumerate(others):
        copies.append(remote(m_ref.at[j], m_out.at[place_at], ms.at[i], mr.at[i], base + j))
        copies.append(
            remote(part(x_ref, j), part(x_out, place_at), xs.at[i], xr.at[i], base + j)
        )
    for copy in copies:
        copy.start()
    mine = [
        pltpu.make_async_copy(part(x_ref, place_at), part(x_out, place_at), own.at[0]),
        pltpu.make_async_copy(m_ref.at[place_at], m_out.at[place_at], own.at[1]),
    ]
    for copy in mine:
        copy.start()
    for copy in mine:
        copy.wait()
    for copy in copies:
        copy.wait_recv()
    for copy in copies:
        copy.wait_send()


def exchange(x, marks, devices):
    dma = pltpu.SemaphoreType.DMA
    return pl.pallas_call(
        functools.partial(exchange_kernel, devices),
        out_shape=[
            jax.ShapeDtypeStruct(x.shape, x.dtype),
            jax.ShapeDtypeStruct(marks.shape, marks.dtype),
        ],
        in_specs=[ANY, ANY],
        out_specs=[ANY, ANY],
        scratch_shapes=[dma((2,))] + [dma((devices // 2,))] * 4,
        compiler_params=pltpu.CompilerParams(collective_id=1, has_side_effects=True),
    )(x, marks)


def place_kernel(devices, aux_ref, got_ref, dense_ref, sums):
    half = devices // 2
    blk = sums.shape[1]
    tile = got_ref.shape[2]
    side = lax.div(lax.axis_index("row"), half)
    sums[...] = jnp.zeros_like(sums)

    def add(p, carry):
        for h in range(2):
            local = (side if h == 0 else 1 - side) * blk * CAP
            for b in range(blk):
                for r in range(CAP):
                    k = local + b * CAP + r
                    a = aux_ref[p, 0, k]
                    sums[h, b, a] += got_ref[p * 2 * blk * CAP + k].astype(jnp.float32)
        return carry

    lax.fori_loop(0, half, add, 0)
    for h in range(2):
        for b in range(blk):
            for a in range(AUX):
                dense_ref[h, pl.ds(a * OI, OI), pl.ds(b * tile, tile)] = sums[h, b, a].astype(
                    jnp.bfloat16
                )


def place(aux, got, devices, blk):
    tile = got.shape[2]
    return pl.pallas_call(
        functools.partial(place_kernel, devices),
        out_shape=jax.ShapeDtypeStruct((2, AUX * OI, blk * tile), jnp.bfloat16),
        in_specs=[SMEM, VMEM],
        out_specs=VMEM,
        scratch_shapes=[pltpu.VMEM((2, blk, AUX + 1, OI, tile), jnp.float32)],
        compiler_params=pltpu.CompilerParams(vmem_limit_bytes=LIMIT),
    )(aux, got)


def reduce_kernel(
    devices, dense_ref, here_ref, there_ref, out_ref,
    parts, near, held_y, far_y, held_z, far_z, a_s, a_r, b_s, b_r, c_s, c_r,
):
    me = lax.axis_index("row")
    depth = devices // 4
    rows = out_ref.shape[0]
    z, y, core = me // 4, (me // 2) % 2, me % 2
    f32, bf16 = jnp.float32, jnp.bfloat16

    def index(zz, yy, cc):
        return (zz * 2 + yy) * 2 + cc

    over_y, over_core = index(z, 1 - y, core), index(z, y, 1 - core)
    to = [(z + i) % depth for i in range(1, depth)] + [z]
    z_peers = [index(zz, y, core) for zz in to[:-1]]
    greet(z_peers + [over_y, over_core])
    turn = (((1,), (1,)), ((), ()))
    a_copies, b_copies, c_copies = [], [], []

    def to_y(i):
        zz = to[i]
        a_copies[2 * i].wait_recv()
        held_y[zz] = (
            parts[zz, 1 - y, core].astype(f32) + near[zz, 1 - y].astype(f32)
        ).astype(bf16)
        copy = remote(held_y.at[zz], far_y.at[zz], b_s.at[i], b_r.at[i], over_y)
        copy.start()
        b_copies.append(copy)

    for i, zz in enumerate(to):
        whole = lax.dot_general(here_ref[zz], dense_ref[0], turn, preferred_element_type=f32)
        whole += lax.dot_general(there_ref[zz], dense_ref[1], turn, preferred_element_type=f32)
        parts[zz] = whole.astype(bf16).reshape(2, 2, rows, whole.shape[1])
        for k, yy in enumerate((1 - y, y)):
            copy = remote(
                parts.at[zz, yy, 1 - core], near.at[zz, yy],
                a_s.at[2 * i + k], a_r.at[2 * i + k], over_core,
            )
            copy.start()
            a_copies.append(copy)
        if i:
            to_y(i - 1)
    to_y(depth - 1)
    for i, zz in enumerate(to):
        a_copies[2 * i + 1].wait_recv()
        b_copies[i].wait_recv()
        total = (
            parts[zz, y, core].astype(f32) + near[zz, y].astype(f32) + far_y[zz].astype(f32)
        )
        if i == depth - 1:
            out_ref[...] = total
        else:
            held_z[zz] = total.astype(bf16)
            copy = remote(held_z.at[zz], far_z.at[z], c_s.at[i], c_r.at[i], z_peers[i])
            copy.start()
            c_copies.append(copy)
    for i in range(1, depth):
        c_copies[i - 1].wait_recv()
        out_ref[...] += far_z[(z + depth - i) % depth].astype(f32)
    for copy in a_copies + b_copies + c_copies:
        copy.wait_send()


def reduce(dense, here, there, devices):
    depth = devices // 4
    rows = here.shape[1] // 4
    wide = dense.shape[1]
    dma = pltpu.SemaphoreType.DMA

    def slots(*lead):
        return pltpu.VMEM(lead + (rows, wide), jnp.bfloat16)

    return pl.pallas_call(
        functools.partial(reduce_kernel, devices),
        out_shape=jax.ShapeDtypeStruct((rows, wide), jnp.float32),
        in_specs=[VMEM] * 3,
        out_specs=VMEM,
        scratch_shapes=[slots(depth, 2, 2), slots(depth, 2)]
        + [slots(depth)] * 4
        + [dma((2 * depth,))] * 2
        + [dma((depth,))] * 4,
        compiler_params=pltpu.CompilerParams(
            collective_id=2, has_side_effects=True, vmem_limit_bytes=LIMIT
        ),
    )(dense, here, there)


def on_device(devices, tiles, tile_row, tile_col, tile_aux, coeffs):
    tile = tiles.shape[1]
    rows, occupied = coeffs.shape
    half, depth = devices // 2, devices // 4
    here = coeffs.T.reshape(depth, occupied // depth, rows)
    there = lax.ppermute(here, "row", [(i, (i + half) % devices) for i in range(devices)])
    own = coeffs[:, :OI].reshape(rows // tile, tile, OI).transpose(0, 2, 1)
    batch = gather(own, devices)
    packed, marks = lefts(tile_row, tile_col, tile_aux, batch, tiles, devices)
    got, got_marks = exchange(packed, marks, devices)
    dense = place(got_marks, got, devices, rows // tile)
    total = reduce(dense, here, there, devices)
    return total.T.reshape(AUX, OI, occupied // devices)


def solution(mesh):
    placed = (
        P(("groups", "row"), None, None),
        P(("groups", "row"), None),
        P(("groups", "row"), None),
        P(("groups", "row")),
        P(("groups", "row"), None),
    )
    return jax.shard_map(
        functools.partial(on_device, mesh.shape["row"]),
        mesh=mesh, in_specs=placed, out_specs=P("groups", None, "row"), check_vma=False,
    )
```

time: 156 us -> 150 us (0.962)
  the two profiles are of different devices: /device:TPU:14 before, /device:TPU:0 now
where the time goes in v2:
time: 150 us
  Pallas kernels  139 us (93%)
  local copies, waits for them, and re-layouts  6.72 us (4%)
  starting transfers between devices  4.1 us (3%)
    pallas_call x1, Pallas kernels, gather(): pl.pallas_call(functools.partial(gather_kernel, devices), out_shape=jax.S...  58.4 us
    pallas_call x1, Pallas kernels, reduce(): pl.pallas_call(functools.partial(reduce_kernel, devices), out_shape=jax.S...  35.5 us
    pallas_call x1, Pallas kernels, exchange(): pl.pallas_call(functools.partial(exchange_kernel, devices), out_shape=[ja...  35.5 us
    pallas_call x1, Pallas kernels, lefts(): pl.pallas_call(functools.partial(left_kernel, devices), out_shape=[jax.Sh...  5.96 us
    ppermute x1, starting transfers between devices, on_device(): lax.ppermute(here, 'row', [(i, (i + half) % devices) for i in range(devic...  4.1 us
    pallas_call x1, Pallas kernels, place(): pl.pallas_call(functools.partial(place_kernel, devices), out_shape=jax.Sh...  3.8 us
    unnamed x14, local copies, waits for them, and re-layouts  3.03 us
  transfers between devices with their start and end apart: 1, of which 0 were waited for; matrix products, arithmetic and copies ran while one was open for 1% of the time, Pallas kernels for 69%

profile of v2, /device:TPU:0, one launch (start us, length us, event | category | flops | bytes accessed | tf_op | source)
XLA Modules:
  0.0 150.1 jit_solution(2422209687399493644)
XLA Ops:
  0.0 0.0 copy-start.4
  0.0 0.0 copy-start.5
  0.0 0.0 copy-start.3
  0.0 1.5 %copy.14 = bf16[1024,512]{1,0:T(8,128)(2,1)S(1)} copy(bf16[1024,512]{0,1:T(8,128)(2,1)} %bitcast.11) | data formatting | bytes 2097152 | tf_op jit(solution)/shard_map/transpose | solution.py:335
  1.5 4.1 %collective-permute-start = (bf16[4,256,512]{2,1,0:T(8,128)(2,1)S(1)}, bf16[4,256,512]{2,1,0:T(8,128)(2,1)}, u32[]{:S(2)}, u32[]{:S(2)}) collective-permute-start(bf16[4,256,512]{2,1,0:T(8,128)(2,1)S(1)} %bitcast.7), channel_id=1, source_target_pairs={{0,8},{1,9},{2,10},{3,11},{4,12},{5,13},{6,14},{7,15},{8,0},{9,1},... | collective-permute-start | bytes 3145736 | tf_op jit(solution)/shard_map/ppermute | solution.py:336
  5.6 0.9 slice.3
  6.6 0.1 copy.11
  6.7 58.4 %shard_map.55.batch_ref = bf16[64,96,128]{2,1,0:T(8,128)(2,1)S(1)} custom-call(bf16[4,96,128]{2,1,0:T(8,128)(2,1)S(1)} %bitcast.10), custom_call_target="tpu_custom_call" | custom-call | tf_op jit(solution)/shard_map/pallas_call | solution.py:88
  65.1 0.0 copy-done.4
  65.1 0.1 copy.12.row_ref
  65.2 0.0 copy-done.5
  65.2 0.1 copy.13.col_ref
  65.3 0.0 copy-done.3
  65.3 0.0 copy-start
  65.3 1.6 %copy-done = bf16[64,128,128]{2,1,0:T(8,128)(2,1)S(1)} copy-done((bf16[64,128,128]{2,1,0:T(8,128)(2,1)S(1)}, bf16[64,128,128]{2,1,0:T(8,128)(2,1)}, u32[]{:S(2)}) %copy-start) | copy-done | bytes 2097176
  66.9 6.0 %shard_map.56 = (bf16[128,96,128]{2,1,0:T(8,128)(2,1)}, s32[8,1,128]{2,1,0:T(1,128)S(1)}) custom-call(s32[64,1]{1,0:T(8,128)S(1)} %copy.12.row_ref, s32[64,1]{1,0:T(8,128)S(1)} %copy.13.col_ref, s32[64]{0:T(128)S(1)} %copy-done.3, bf16[64,96,128]{2,1,0:T(8,128)(2,1)S(1)} %shard_map.55.batch_ref, bf16[64,128,128]{2,1,0:T(8,128)(2,1)S(1)} %copy-done), custom_call_target="tpu_custom_call" | custom-call | tf_op jit(solution)/shard_map/pallas_call | solution.py:144
  72.9 0.0 copy-start.1
  72.9 0.6 copy-done.1
  73.5 35.5 %shard_map.57 = (bf16[128,96,128]{2,1,0:T(8,128)(2,1)}, s32[8,1,128]{2,1,0:T(1,128)}) custom-call(bf16[128,96,128]{2,1,0:T(8,128)(2,1)} %get-tuple-element.9.x_ref, s32[8,1,128]{2,1,0:T(1,128)} %copy-done.1), custom_call_target="tpu_custom_call" | custom-call | tf_op jit(solution)/shard_map/pallas_call | solution.py:192
  109.0 0.0 copy-start.2
  109.0 0.7 copy-done.2
  109.6 3.8 %shard_map.58.dense_ref = bf16[2,1536,512]{2,1,0:T(8,128)(2,1)S(1)} custom-call(s32[8,1,128]{2,1,0:T(1,128)S(1)} %copy-done.2, bf16[128,96,128]{2,1,0:T(8,128)(2,1)} %get-tuple-element.12.got_ref), custom_call_target="tpu_custom_call" | custom-call | tf_op jit(solution)/shard_map/pallas_call | solution.py:233
  113.4 0.0 collective-permute-done.there_ref
  113.4 35.5 %shard_map.59 = f32[64,1536]{1,0:T(8,128)S(1)} custom-call(bf16[2,1536,512]{2,1,0:T(8,128)(2,1)S(1)} %shard_map.58.dense_ref, bf16[4,256,512]{2,1,0:T(8,128)(2,1)S(1)} %bitcast.8, bf16[4,256,512]{2,1,0:T(8,128)(2,1)} %collective-permute-done.there_ref), custom_call_target="tpu_custom_call" | custom-call | tf_op jit(solution)/shard_map/pallas_call | solution.py:316
  149.0 0.2 reshape.11
  149.2 1.0 copy.15
Async XLA Ops:
  0.0 65.1 %copy-start.4 = (s32[64,1]{0,1:T(1,128)S(1)}, s32[64,1]{0,1:T(1,128)}, u32[]{:S(2)}) copy-start(s32[64,1]{0,1:T(1,128)} %param.6) | copy-start | bytes 772
  0.0 65.2 %copy-start.5 = (s32[64,1]{0,1:T(1,128)S(1)}, s32[64,1]{0,1:T(1,128)}, u32[]{:S(2)}) copy-start(s32[64,1]{0,1:T(1,128)} %param.7) | copy-start | bytes 772
  0.0 65.3 %copy-start.3 = (s32[64]{0:T(128)S(1)}, s32[64]{0:T(128)}, u32[]{:S(2)}) copy-start(s32[64]{0:T(128)} %aux_ref.1) | copy-start | bytes 772
  1.5 111.9 %collective-permute-start = (bf16[4,256,512]{2,1,0:T(8,128)(2,1)S(1)}, bf16[4,256,512]{2,1,0:T(8,128)(2,1)}, u32[]{:S(2)}, u32[]{:S(2)}) collective-permute-start(bf16[4,256,512]{2,1,0:T(8,128)(2,1)S(1)} %bitcast.7), channel_id=1, source_target_pairs={{0,8},{1,9},{2,10},{3,11},{4,12},{5,13},{6,14},{7,15},{8,0},{9,1},... | collective-permute-start | bytes 3145736 | tf_op jit(solution)/shard_map/ppermute | solution.py:336
  65.3 1.6 %copy-start = (bf16[64,128,128]{2,1,0:T(8,128)(2,1)S(1)}, bf16[64,128,128]{2,1,0:T(8,128)(2,1)}, u32[]{:S(2)}) copy-start(bf16[64,128,128]{2,1,0:T(8,128)(2,1)} %tiles_ref.1) | copy-start | bytes 6291460
  72.9 0.6 copy-start.1
  109.0 0.7 copy-start.2

commit v3 on v2

--- a/solution.py
+++ b/solution.py
@@ -333,9 +333,10 @@
     rows, occupied = coeffs.shape
     half, depth = devices // 2, devices // 4
     here = coeffs.T.reshape(depth, occupied // depth, rows)
-    there = lax.ppermute(here, "row", [(i, (i + half) % devices) for i in range(devices)])
     own = coeffs[:, :OI].reshape(rows // tile, tile, OI).transpose(0, 2, 1)
     batch = gather(own, devices)
+    here, batch = lax.optimization_barrier((here, batch))
+    there = lax.ppermute(here, "row", [(i, (i + half) % devices) for i in range(devices)])
     packed, marks = lefts(tile_row, tile_col, tile_aux, batch, tiles, devices)
     got, got_marks = exchange(packed, marks, devices)
     dense = place(got_marks, got, devices, rows // tile)

time: 150 us -> 128 us (0.85)
  Pallas kernels: 139 us -> 118 us
  starting transfers between devices: 4.1 us -> 2.59 us
    pallas_call x1, Pallas kernels: 58.4 us -> 19.9 us  [gather(): pl.pallas_call(functools.partial(gather_kernel, devices), out_shape=jax.S...]
    pallas_call x1, Pallas kernels: 35.5 us -> 48.8 us  [exchange(): pl.pallas_call(functools.partial(exchange_kernel, devices), out_shape=[ja...]
    pallas_call x1, Pallas kernels: 35.5 us -> 39.9 us  [reduce(): pl.pallas_call(functools.partial(reduce_kernel, devices), out_shape=jax.S...]
    ppermute x1, starting transfers between devices: 4.1 us -> 2.59 us  [on_device(): lax.ppermute(here, 'row', [(i, (i + half) % devices) for i in range(devic...]
  transfers between devices with their start and end apart: 1 -> 1, of which waited for: 0 -> 0; matrix products, arithmetic and copies ran while one was open for 1% -> 0% of each run, Pallas kernels for 69% -> 46%
where the time goes in v3:
time: 128 us
  Pallas kernels  118 us (92%)
  local copies, waits for them, and re-layouts  6.72 us (5%)
  starting transfers between devices  2.59 us (2%)
    pallas_call x1, Pallas kernels, exchange(): pl.pallas_call(functools.partial(exchange_kernel, devices), out_shape=[ja...  48.8 us
    pallas_call x1, Pallas kernels, reduce(): pl.pallas_call(functools.partial(reduce_kernel, devices), out_shape=jax.S...  39.9 us
    pallas_call x1, Pallas kernels, gather(): pl.pallas_call(functools.partial(gather_kernel, devices), out_shape=jax.S...  19.9 us
    pallas_call x1, Pallas kernels, lefts(): pl.pallas_call(functools.partial(left_kernel, devices), out_shape=[jax.Sh...  5.95 us
    pallas_call x1, Pallas kernels, place(): pl.pallas_call(functools.partial(place_kernel, devices), out_shape=jax.Sh...  3.8 us
    unnamed x14, local copies, waits for them, and re-layouts  3.03 us
    ppermute x1, starting transfers between devices, on_device(): lax.ppermute(here, 'row', [(i, (i + half) % devices) for i in range(devic...  2.59 us
  transfers between devices with their start and end apart: 1, of which 0 were waited for; matrix products, arithmetic and copies ran while one was open for 0% of the time, Pallas kernels for 46%

profile of v3, /device:TPU:0, one launch (start us, length us, event | category | flops | bytes accessed | tf_op | source)
XLA Modules:
  0.0 127.7 jit_solution(1428203704634030478)
XLA Ops:
  0.0 0.0 copy-start.4
  0.0 0.0 copy-start.5
  0.0 0.0 copy-start.3
  0.0 1.0 slice.3
  1.0 0.1 copy.12
  1.1 19.9 %shard_map.55.batch_ref = bf16[64,96,128]{2,1,0:T(8,128)(2,1)S(1)} custom-call(bf16[4,96,128]{2,1,0:T(8,128)(2,1)S(1)} %bitcast.10), custom_call_target="tpu_custom_call" | custom-call | tf_op jit(solution)/shard_map/pallas_call | solution.py:88
  21.0 1.5 %copy.10 = bf16[1024,512]{1,0:T(8,128)(2,1)S(1)} copy(bf16[1024,512]{0,1:T(8,128)(2,1)} %bitcast.11) | data formatting | bytes 2097152 | tf_op jit(solution)/shard_map/transpose | solution.py:335
  22.5 2.6 %collective-permute-start = (bf16[4,256,512]{2,1,0:T(8,128)(2,1)S(1)}, bf16[4,256,512]{2,1,0:T(8,128)(2,1)}, u32[]{:S(2)}, u32[]{:S(2)}) collective-permute-start(bf16[4,256,512]{2,1,0:T(8,128)(2,1)S(1)} %bitcast.7), channel_id=1, source_target_pairs={{0,8},{1,9},{2,10},{3,11},{4,12},{5,13},{6,14},{7,15},{8,0},{9,1},... | collective-permute-start | bytes 3145736 | tf_op jit(solution)/shard_map/ppermute | solution.py:339
  25.1 0.0 copy-done.4
  25.1 0.1 copy.13.row_ref
  25.2 0.0 copy-done.5
  25.2 0.1 copy.14.col_ref
  25.3 0.0 copy-done.3
  25.3 0.0 copy-start
  25.3 1.6 %copy-done = bf16[64,128,128]{2,1,0:T(8,128)(2,1)S(1)} copy-done((bf16[64,128,128]{2,1,0:T(8,128)(2,1)S(1)}, bf16[64,128,128]{2,1,0:T(8,128)(2,1)}, u32[]{:S(2)}) %copy-start) | copy-done | bytes 2097176
  26.9 6.0 %shard_map.56 = (bf16[128,96,128]{2,1,0:T(8,128)(2,1)}, s32[8,1,128]{2,1,0:T(1,128)S(1)}) custom-call(s32[64,1]{1,0:T(8,128)S(1)} %copy.13.row_ref, s32[64,1]{1,0:T(8,128)S(1)} %copy.14.col_ref, s32[64]{0:T(128)S(1)} %copy-done.3, bf16[64,96,128]{2,1,0:T(8,128)(2,1)S(1)} %shard_map.55.batch_ref, bf16[64,128,128]{2,1,0:T(8,128)(2,1)S(1)} %copy-done), custom_call_target="tpu_custom_call" | custom-call | tf_op jit(solution)/shard_map/pallas_call | solution.py:144
  32.8 0.0 copy-start.1
  32.8 0.6 copy-done.1
  33.4 48.8 %shard_map.57 = (bf16[128,96,128]{2,1,0:T(8,128)(2,1)}, s32[8,1,128]{2,1,0:T(1,128)}) custom-call(bf16[128,96,128]{2,1,0:T(8,128)(2,1)} %get-tuple-element.12.x_ref, s32[8,1,128]{2,1,0:T(1,128)} %copy-done.1), custom_call_target="tpu_custom_call" | custom-call | tf_op jit(solution)/shard_map/pallas_call | solution.py:192
  82.2 0.0 copy-start.2
  82.2 0.7 copy-done.2
  82.9 3.8 %shard_map.58.dense_ref = bf16[2,1536,512]{2,1,0:T(8,128)(2,1)S(1)} custom-call(s32[8,1,128]{2,1,0:T(1,128)S(1)} %copy-done.2, bf16[128,96,128]{2,1,0:T(8,128)(2,1)} %get-tuple-element.15.got_ref), custom_call_target="tpu_custom_call" | custom-call | tf_op jit(solution)/shard_map/pallas_call | solution.py:233
  86.7 0.0 collective-permute-done.there_ref
  86.7 39.9 %shard_map.59 = f32[64,1536]{1,0:T(8,128)S(1)} custom-call(bf16[2,1536,512]{2,1,0:T(8,128)(2,1)S(1)} %shard_map.58.dense_ref, bf16[4,256,512]{2,1,0:T(8,128)(2,1)S(1)} %bitcast.8, bf16[4,256,512]{2,1,0:T(8,128)(2,1)} %collective-permute-done.there_ref), custom_call_target="tpu_custom_call" | custom-call | tf_op jit(solution)/shard_map/pallas_call | solution.py:316
  126.6 0.2 reshape.11
  126.7 1.0 copy.15
Async XLA Ops:
  0.0 25.1 %copy-start.4 = (s32[64,1]{0,1:T(1,128)S(1)}, s32[64,1]{0,1:T(1,128)}, u32[]{:S(2)}) copy-start(s32[64,1]{0,1:T(1,128)} %param.6) | copy-start | bytes 772
  0.0 25.2 %copy-start.5 = (s32[64,1]{0,1:T(1,128)S(1)}, s32[64,1]{0,1:T(1,128)}, u32[]{:S(2)}) copy-start(s32[64,1]{0,1:T(1,128)} %param.7) | copy-start | bytes 772
  0.0 25.3 %copy-start.3 = (s32[64]{0:T(128)S(1)}, s32[64]{0:T(128)}, u32[]{:S(2)}) copy-start(s32[64]{0:T(128)} %aux_ref.1) | copy-start | bytes 772
  22.5 64.2 %collective-permute-start = (bf16[4,256,512]{2,1,0:T(8,128)(2,1)S(1)}, bf16[4,256,512]{2,1,0:T(8,128)(2,1)}, u32[]{:S(2)}, u32[]{:S(2)}) collective-permute-start(bf16[4,256,512]{2,1,0:T(8,128)(2,1)S(1)} %bitcast.7), channel_id=1, source_target_pairs={{0,8},{1,9},{2,10},{3,11},{4,12},{5,13},{6,14},{7,15},{8,0},{9,1},... | collective-permute-start | bytes 3145736 | tf_op jit(solution)/shard_map/ppermute | solution.py:339
  25.3 1.6 %copy-start = (bf16[64,128,128]{2,1,0:T(8,128)(2,1)S(1)}, bf16[64,128,128]{2,1,0:T(8,128)(2,1)}, u32[]{:S(2)}) copy-start(bf16[64,128,128]{2,1,0:T(8,128)(2,1)} %tiles_ref.1) | copy-start | bytes 6291460
  32.8 0.6 copy-start.1
  82.2 0.7 copy-start.2

commit v4 on v2

v4 whole, which is shorter than its diff:
```python
import functools
import jax
import jax.numpy as jnp
from jax import lax
from jax.experimental import pallas as pl
from jax.experimental.pallas import tpu as pltpu
from jax.sharding import PartitionSpec as P

OI = 96
AUX = 16
CAP = 2
MESH = pl.DeviceIdType.MESH
VMEM = pl.BlockSpec(memory_space=pltpu.VMEM)
SMEM = pl.BlockSpec(memory_space=pltpu.SMEM)
ANY = pl.BlockSpec(memory_space=pl.ANY)
LIMIT = 48 * 1024 * 1024


def greet(peers):
    barrier = pltpu.get_barrier_semaphore()
    for peer in peers:
        pl.semaphore_signal(barrier, inc=1, device_id={"row": peer}, device_id_type=MESH)
    pl.semaphore_wait(barrier, len(peers))


def remote(src, dst, send, recv, peer):
    return pltpu.make_async_remote_copy(
        src_ref=src, dst_ref=dst, send_sem=send, recv_sem=recv,
        device_id={"row": peer}, device_id_type=MESH,
    )


def slots_kernel(devices, blk, col_ref, aux_ref, pick_ref, marks_ref, seen_ref):
    half = devices // 2
    per = 2 * blk * CAP
    for b in range(devices * blk):
        seen_ref[b] = 0
    for j in range(half):
        for k in range(per):
            marks_ref[j, 0, k] = AUX
            pick_ref[j * per + k] = 0

    def step(t, carry):
        c = col_ref[t]
        rank = seen_ref[c]
        seen_ref[c] = rank + 1
        dev = lax.div(c, blk)
        dest = lax.rem(dev, half)
        at = (lax.div(dev, half) * blk + lax.rem(c, blk)) * CAP + rank
        pick_ref[dest * per + at] = t
        marks_ref[dest, 0, at] = aux_ref[t]
        return carry

    lax.fori_loop(0, col_ref.shape[0], step, 0, unroll=4)


def choose_slots(tile_col, tile_aux, devices, blk):
    blocks = devices * blk
    return pl.pallas_call(
        functools.partial(slots_kernel, devices, blk),
        out_shape=[
            jax.ShapeDtypeStruct((blocks * CAP,), jnp.int32),
            jax.ShapeDtypeStruct((devices // 2, 1, 128), jnp.int32),
        ],
        in_specs=[SMEM, SMEM],
        out_specs=[SMEM, SMEM],
        scratch_shapes=[pltpu.SMEM((blocks,), jnp.int32)],
    )(tile_col, tile_aux)


def build_kernel(
    devices, row_ref, pick_ref, own_ref, tiles_ref, here_ref, m_ref,
    got_ref, m_out, there_ref,
    batch_ref, send_ref, zs, zr, ys, yr, cs, cr, hs, hr, xs, xr, ms, mr, local,
):
    me = lax.axis_index("row")
    blk = own_ref.shape[0]
    depth, half = devices // 4, devices // 2
    deep = depth // 2
    z, y, core = me // 4, (me // 2) % 2, me % 2
    side, place_at = me // half, me % half
    per = 2 * blk * CAP

    def index(zz, yy, cc):
        return (zz * 2 + yy) * 2 + cc

    def at(dev):
        return batch_ref.at[pl.ds(dev * blk, blk)]

    def part(ref, j):
        return ref.at[pl.ds(j * per, per)]

    z_peers = [index((z + i) % depth, y, core) for i in range(1, depth)]
    over_y, over_core = index(z, 1 - y, core), index(z, y, 1 - core)
    across = (me + half) % devices
    relative = [(dz, a, b) for dz in range(1, deep) for a in range(2) for b in range(2)]
    relative += [(0, 1, 0), (0, 1, 1), (0, 0, 1)]
    targets = [
        index((z % deep + dz) % deep, (y + a) % 2, (core + b) % 2) for dz, a, b in relative
    ]
    greet(
        [side * half + j for j in targets]
        + [index((1 - side) * deep + k, y, core) for k in range(deep)]
    )
    z_copies, y_copies, c_copies, h_copies, x_copies = [], [], [], [], []
    for i, peer in enumerate(z_peers):
        copy = remote(own_ref, at(me), zs.at[i], zr.at[i], peer)
        copy.start()
        z_copies.append(copy)

    def forward(copies, i, dev, send, recv, peer):
        src = own_ref if i == 0 else at(dev)
        copy = remote(src, at(dev), send.at[i], recv.at[i], peer)
        copy.start()
        copies.append(copy)

    forward(y_copies, 0, me, ys, yr, over_y)
    forward(c_copies, 0, me, cs, cr, over_core)
    for i in range(depth):
        copy = remote(here_ref.at[i], there_ref.at[i], hs.at[i], hr.at[i], across)
        copy.start()
        h_copies.append(copy)
    batch_ref[pl.ds(me * blk, blk)] = own_ref[...]
    for i in range(1, depth):
        z_copies[i - 1].wait_recv()
        dev = index((z + depth - i) % depth, y, core)
        forward(y_copies, i, dev, ys, yr, over_y)
        forward(c_copies, i, dev, cs, cr, over_core)
    for i in range(depth):
        y_copies[i].wait_recv()
        dev = index((z + depth - i) % depth, 1 - y, core)
        forward(c_copies, depth + i, dev, cs, cr, over_core)
    for copy in c_copies:
        copy.wait_recv()

    width = min(8, per)

    def fill(ref, j):
        def step(g, carry):
            first = j * per + g * width
            for u in range(width):
                t = pick_ref[first + u]
                ref[first + u] = jnp.dot(
                    batch_ref[row_ref[t]], tiles_ref[t], preferred_element_type=jnp.float32
                ).astype(jnp.bfloat16)
            return carry

        lax.fori_loop(0, per // width, step, 0)

    for i, j in enumerate(targets):
        peer = side * half + j
        fill(send_ref, j)
        x_copies.append(
            remote(part(send_ref, j), part(got_ref, place_at), xs.at[i], xr.at[i], peer)
        )
        x_copies.append(remote(m_ref.at[j], m_out.at[place_at], ms.at[i], mr.at[i], peer))
        x_copies[-2].start()
        x_copies[-1].start()
    mine = pltpu.make_async_copy(m_ref.at[place_at], m_out.at[place_at], local.at[0])
    mine.start()
    fill(got_ref, place_at)
    mine.wait()
    for copy in x_copies + h_copies:
        copy.wait_recv()
    for copy in z_copies + y_copies + c_copies + h_copies + x_copies:
        copy.wait_send()


def build(tile_row, pick, own, tiles, here, marks, devices):
    depth, half = devices // 4, devices // 2
    dma = pltpu.SemaphoreType.DMA
    tile = tiles.shape[1]
    slots = pick.shape[0]
    return pl.pallas_call(
        functools.partial(build_kernel, devices),
        out_shape=[
            jax.ShapeDtypeStruct((slots, OI, tile), jnp.bfloat16),
            jax.ShapeDtypeStruct(marks.shape, marks.dtype),
            jax.ShapeDtypeStruct(here.shape, here.dtype),
        ],
        in_specs=[SMEM, SMEM, VMEM, VMEM, VMEM, ANY],
        out_specs=[VMEM, ANY, VMEM],
        scratch_shapes=[
            pltpu.VMEM((devices * own.shape[0],) + own.shape[1:], own.dtype),
            pltpu.VMEM((slots, OI, tile), jnp.bfloat16),
        ]
        + [dma((depth,))] * 4
        + [dma((2 * depth,))] * 2
        + [dma((depth,))] * 2
        + [dma((half,))] * 4
        + [dma((1,))],
        compiler_params=pltpu.CompilerParams(
            collective_id=0, has_side_effects=True, vmem_limit_bytes=LIMIT
        ),
    )(tile_row, pick, own, tiles, here, marks)


def place_kernel(devices, aux_ref, got_ref, dense_ref, sums):
    half = devices // 2
    blk = sums.shape[1]
    tile = got_ref.shape[2]
    side = lax.div(lax.axis_index("row"), half)
    sums[...] = jnp.zeros_like(sums)

    def add(p, carry):
        for h in range(2):
            local = (side if h == 0 else 1 - side) * blk * CAP
            for b in range(blk):
                for r in range(CAP):
                    k = local + b * CAP + r
                    a = aux_ref[p, 0, k]
                    sums[h, b, a] += got_ref[p * 2 * blk * CAP + k].astype(jnp.float32)
        return carry

    lax.fori_loop(0, half, add, 0)
    for h in range(2):
        for b in range(blk):
            for a in range(AUX):
                dense_ref[h, pl.ds(a * OI, OI), pl.ds(b * tile, tile)] = sums[h, b, a].astype(
                    jnp.bfloat16
                )


def place(aux, got, devices, blk):
    tile = got.shape[2]
    return pl.pallas_call(
        functools.partial(place_kernel, devices),
        out_shape=jax.ShapeDtypeStruct((2, AUX * OI, blk * tile), jnp.bfloat16),
        in_specs=[SMEM, VMEM],
        out_specs=VMEM,
        scratch_shapes=[pltpu.VMEM((2, blk, AUX + 1, OI, tile), jnp.float32)],
        compiler_params=pltpu.CompilerParams(vmem_limit_bytes=LIMIT),
    )(aux, got)


def reduce_kernel(
    devices, dense_ref, here_ref, there_ref, out_ref,
    parts, near, held_y, far_y, held_z, far_z, a_s, a_r, b_s, b_r, c_s, c_r,
):
    me = lax.axis_index("row")
    depth = devices // 4
    rows = out_ref.shape[0]
    z, y, core = me // 4, (me // 2) % 2, me % 2
    f32, bf16 = jnp.float32, jnp.bfloat16

    def index(zz, yy, cc):
        return (zz * 2 + yy) * 2 + cc

    over_y, over_core = index(z, 1 - y, core), index(z, y, 1 - core)
    to = [(z + i) % depth for i in range(1, depth)] + [z]
    z_peers = [index(zz, y, core) for zz in to[:-1]]
    greet(z_peers + [over_y, over_core])
    turn = (((1,), (1,)), ((), ()))
    a_copies, b_copies, c_copies = [], [], []

    def to_y(i):
        zz = to[i]
        a_copies[2 * i].wait_recv()
        held_y[zz] = (
            parts[zz, 1 - y, core].astype(f32) + near[zz, 1 - y].astype(f32)
        ).astype(bf16)
        copy = remote(held_y.at[zz], far_y.at[zz], b_s.at[i], b_r.at[i], over_y)
        copy.start()
        b_copies.append(copy)

    for i, zz in enumerate(to):
        whole = lax.dot_general(here_ref[zz], dense_ref[0], turn, preferred_element_type=f32)
        whole += lax.dot_general(there_ref[zz], dense_ref[1], turn, preferred_element_type=f32)
        parts[zz] = whole.astype(bf16).reshape(2, 2, rows, whole.shape[1])
        for k, yy in enumerate((1 - y, y)):
            copy = remote(
                parts.at[zz, yy, 1 - core], near.at[zz, yy],
                a_s.at[2 * i + k], a_r.at[2 * i + k], over_core,
            )
            copy.start()
            a_copies.append(copy)
        if i:
            to_y(i - 1)
    to_y(depth - 1)
    for i, zz in enumerate(to):
        a_copies[2 * i + 1].wait_recv()
        b_copies[i].wait_recv()
        total = (
            parts[zz, y, core].astype(f32) + near[zz, y].astype(f32) + far_y[zz].astype(f32)
        )
        if i == depth - 1:
            out_ref[...] = total
        else:
            held_z[zz] = total.astype(bf16)
            copy = remote(held_z.at[zz], far_z.at[z], c_s.at[i], c_r.at[i], z_peers[i])
            copy.start()
            c_copies.append(copy)
    for i in range(1, depth):
        c_copies[i - 1].wait_recv()
        out_ref[...] += far_z[(z + depth - i) % depth].astype(f32)
    for copy in a_copies + b_copies + c_copies:
        copy.wait_send()


def reduce(dense, here, there, devices):
    depth = devices // 4
    rows = here.shape[1] // 4
    wide = dense.shape[1]
    dma = pltpu.SemaphoreType.DMA

    def slots(*lead):
        return pltpu.VMEM(lead + (rows, wide), jnp.bfloat16)

    return pl.pallas_call(
        functools.partial(reduce_kernel, devices),
        out_shape=jax.ShapeDtypeStruct((rows, wide), jnp.float32),
        in_specs=[VMEM] * 3,
        out_specs=VMEM,
        scratch_shapes=[slots(depth, 2, 2), slots(depth, 2)]
        + [slots(depth)] * 4
        + [dma((2 * depth,))] * 2
        + [dma((depth,))] * 4,
        compiler_params=pltpu.CompilerParams(
            collective_id=1, has_side_effects=True, vmem_limit_bytes=LIMIT
        ),
    )(dense, here, there)


def on_device(devices, tiles, tile_row, tile_col, tile_aux, coeffs):
    tile = tiles.shape[1]
    rows, occupied = coeffs.shape
    blk, depth = rows // tile, devices // 4
    here = coeffs.T.reshape(depth, occupied // depth, rows)
    own = coeffs[:, :OI].reshape(blk, tile, OI).transpose(0, 2, 1)
    pick, marks = choose_slots(tile_col.reshape(-1), tile_aux, devices, blk)
    got, got_marks, there = build(tile_row.reshape(-1), pick, own, tiles, here, marks, devices)
    dense = place(got_marks, got, devices, blk)
    total = reduce(dense, here, there, devices)
    return total.T.reshape(AUX, OI, occupied // devices)


def solution(mesh):
    placed = (
        P(("groups", "row"), None, None),
        P(("groups", "row"), None),
        P(("groups", "row"), None),
        P(("groups", "row")),
        P(("groups", "row"), None),
    )
    return jax.shard_map(
        functools.partial(on_device, mesh.shape["row"]),
        mesh=mesh, in_specs=placed, out_specs=P("groups", None, "row"), check_vma=False,
    )
```

time: 150 us -> 139 us (0.927)
  Pallas kernels: 139 us -> 133 us
  starting transfers between devices: 4.1 us -> 0 us
    pallas_call x1, Pallas kernels: 35.5 us -> 29 us  [reduce(): pl.pallas_call(functools.partial(reduce_kernel, devices), out_shape=jax.S...]
    ppermute x1 -> x0, starting transfers between devices: 4.1 us -> none  [on_device(): lax.ppermute(here, 'row', [(i, (i + half) % devices) for i in range(devic...]
    unnamed x14 -> x8, local copies, waits for them, and re-layouts: 3.03 us -> 1.94 us
    pallas_call x3 -> x2, Pallas kernels: 99.9 us -> 100 us  [the longest x1 97.7 us: build(): pl.pallas_call(functools.partial(build_kernel, devices), out_shape=[jax.S...]
  transfers between devices with their start and end apart: 1 -> 0, of which waited for: 0 -> 0; matrix products, arithmetic and copies ran while one was open for 1% -> 0% of each run, Pallas kernels for 69% -> 0%
where the time goes in v4:
time: 139 us
  Pallas kernels  133 us (96%)
  local copies, waits for them, and re-layouts  5.59 us (4%)
    pallas_call x1, Pallas kernels, build(): pl.pallas_call(functools.partial(build_kernel, devices), out_shape=[jax.S...  97.7 us
    pallas_call x1, Pallas kernels, reduce(): pl.pallas_call(functools.partial(reduce_kernel, devices), out_shape=jax.S...  29 us
    pallas_call x1, Pallas kernels, place(): pl.pallas_call(functools.partial(place_kernel, devices), out_shape=jax.Sh...  3.81 us

profile of v4, /device:TPU:0, one launch (start us, length us, event | category | flops | bytes accessed | tf_op | source)
XLA Modules:
  0.0 138.6 jit_solution(5305109139425212843)
XLA Ops:
  0.0 0.0 copy-start
  0.0 2.3 %shard_map.55 = (s32[128]{0:T(128)}, s32[8,1,128]{2,1,0:T(1,128)}) custom-call(s32[64]{0:T(128)} %bitcast.16, s32[64]{0:T(128)} %aux_ref.1), custom_call_target="tpu_custom_call" | custom-call | tf_op jit(solution)/shard_map/pallas_call | solution.py:59
  2.3 0.9 slice.3
  3.3 0.1 copy.9
  3.4 1.5 %copy.10 = bf16[1024,512]{1,0:T(8,128)(2,1)S(1)} copy(bf16[1024,512]{0,1:T(8,128)(2,1)} %bitcast.14) | data formatting | bytes 2097152 | tf_op jit(solution)/shard_map/transpose | solution.py:328
  4.9 0.0 copy-done
  4.9 0.0 copy-start.1
  4.9 0.7 copy-done.1
  5.6 0.0 copy-start.2
  5.6 0.7 copy-done.2
  6.2 0.0 copy-start.3
  6.2 0.6 copy-done.3
  6.8 97.7 %shard_map.56 = (bf16[128,96,128]{2,1,0:T(8,128)(2,1)}, s32[8,1,128]{2,1,0:T(1,128)S(1)}, bf16[4,256,512]{2,1,0:T(8,128)(2,1)S(1)}) custom-call(s32[64]{0:T(128)S(1)} %bitcast.13, s32[128]{0:T(128)S(1)} %copy-done.3, bf16[4,96,128]{2,1,0:T(8,128)(2,1)S(1)} %bitcast.12, bf16[64,128,128]{2,1,0:T(8,128)(2,1)S(1)} %copy-done, bf16[4,256,512]{2,1,0:T(8,128)(2,1)S(1)} %bitcast.9, ...), custom_call_target="tpu_custom_call" | custom-call | tf_op jit(solution)/shard_map/pallas_call | solution.py:174
  104.6 3.8 %shard_map.57.dense_ref = bf16[2,1536,512]{2,1,0:T(8,128)(2,1)S(1)} custom-call(s32[8,1,128]{2,1,0:T(1,128)S(1)} %get-tuple-element.12.aux_ref, bf16[128,96,128]{2,1,0:T(8,128)(2,1)} %get-tuple-element.13.got_ref), custom_call_target="tpu_custom_call" | custom-call | tf_op jit(solution)/shard_map/pallas_call | solution.py:226
  108.4 29.0 %shard_map.58 = f32[64,1536]{1,0:T(8,128)S(1)} custom-call(bf16[2,1536,512]{2,1,0:T(8,128)(2,1)S(1)} %shard_map.57.dense_ref, bf16[4,256,512]{2,1,0:T(8,128)(2,1)S(1)} %bitcast.10, bf16[4,256,512]{2,1,0:T(8,128)(2,1)S(1)} %get-tuple-element.14.there_ref), custom_call_target="tpu_custom_call" | custom-call | tf_op jit(solution)/shard_map/pallas_call | solution.py:309
  137.5 0.2 reshape.19
  137.6 1.0 copy.11
Async XLA Ops:
  0.0 4.9 %copy-start = (bf16[64,128,128]{2,1,0:T(8,128)(2,1)S(1)}, bf16[64,128,128]{2,1,0:T(8,128)(2,1)}, u32[]{:S(2)}) copy-start(bf16[64,128,128]{2,1,0:T(8,128)(2,1)} %tiles_ref.1) | copy-start | bytes 6291460
  4.9 0.7 copy-start.1
  5.6 0.7 copy-start.2
  6.2 0.6 copy-start.3

commit v5 on v4

--- a/solution.py
+++ b/solution.py
@@ -13,6 +13,7 @@
 VMEM = pl.BlockSpec(memory_space=pltpu.VMEM)
 SMEM = pl.BlockSpec(memory_space=pltpu.SMEM)
 ANY = pl.BlockSpec(memory_space=pl.ANY)
+EARLY = 1
 LIMIT = 48 * 1024 * 1024
 
 
@@ -30,47 +31,41 @@
     )
 
 
-def slots_kernel(devices, blk, col_ref, aux_ref, pick_ref, marks_ref, seen_ref):
+def log2(size):
+    return size.bit_length() - 1
+
+
+def choose_slots(devices, blk, row_ref, col_ref, aux_ref):
+    count = col_ref.shape[1]
     half = devices // 2
     per = 2 * blk * CAP
-    for b in range(devices * blk):
-        seen_ref[b] = 0
-    for j in range(half):
-        for k in range(per):
-            marks_ref[j, 0, k] = AUX
-            pick_ref[j * per + k] = 0
-
-    def step(t, carry):
-        c = col_ref[t]
-        rank = seen_ref[c]
-        seen_ref[c] = rank + 1
-        dev = lax.div(c, blk)
-        dest = lax.rem(dev, half)
-        at = (lax.div(dev, half) * blk + lax.rem(c, blk)) * CAP + rank
-        pick_ref[dest * per + at] = t
-        marks_ref[dest, 0, at] = aux_ref[t]
-        return carry
-
-    lax.fori_loop(0, col_ref.shape[0], step, 0, unroll=4)
-
-
-def choose_slots(tile_col, tile_aux, devices, blk):
-    blocks = devices * blk
-    return pl.pallas_call(
-        functools.partial(slots_kernel, devices, blk),
-        out_shape=[
-            jax.ShapeDtypeStruct((blocks * CAP,), jnp.int32),
-            jax.ShapeDtypeStruct((devices // 2, 1, 128), jnp.int32),
-        ],
-        in_specs=[SMEM, SMEM],
-        out_specs=[SMEM, SMEM],
-        scratch_shapes=[pltpu.SMEM((blocks,), jnp.int32)],
-    )(tile_col, tile_aux)
+    slots = half * per
+    down = lax.broadcasted_iota(jnp.int32, (count, count), 0)
+    right = lax.broadcasted_iota(jnp.int32, (count, count), 1)
+
+    def upright(ref):
+        return jnp.sum(jnp.where(down == right, ref[...], 0), axis=1, keepdims=True)
+
+    rows, cols, auxes = upright(row_ref), upright(col_ref), upright(aux_ref)
+    earlier = jnp.logical_and(cols == col_ref[...], right < down)
+    rank = jnp.sum(jnp.where(earlier, 1, 0), axis=1, keepdims=True)
+    dev = lax.shift_right_logical(cols, jnp.full_like(cols, log2(blk)))
+    dest = dev & (half - 1)
+    upper = lax.shift_right_logical(dev, jnp.full_like(dev, log2(half)))
+    slot = dest * per + (upper * blk + (cols & (blk - 1))) * CAP + rank
+    hit = slot == lax.broadcasted_iota(jnp.int32, (count, slots), 1)
+    which = lax.broadcasted_iota(jnp.int32, (count, slots), 0)
+
+    def chosen(values):
+        return jnp.sum(jnp.where(hit, values, 0), axis=0, keepdims=True)
+
+    return chosen(which), chosen(rows), chosen(auxes - AUX) + AUX
 
 
 def build_kernel(
-    devices, row_ref, pick_ref, own_ref, tiles_ref, here_ref, m_ref,
-    got_ref, m_out, there_ref,
+    devices, row_ref, col_ref, aux_ref, coeffs_ref, tiles_hbm,
+    got_ref, m_out, here_ref, there_ref,
+    own_ref, tiles_ref, slot_ref, m_ref, pick_ref, at_row_ref,
     batch_ref, send_ref, zs, zr, ys, yr, cs, cr, hs, hr, xs, xr, ms, mr, local,
 ):
     me = lax.axis_index("row")
@@ -98,10 +93,15 @@
     targets = [
         index((z % deep + dz) % deep, (y + a) % 2, (core + b) % 2) for dz, a, b in relative
     ]
+    tile = own_ref.shape[2]
+    for b in range(blk):
+        own_ref[b] = coeffs_ref[pl.ds(b * tile, tile), pl.ds(0, 128)].T[:OI]
     greet(
         [side * half + j for j in targets]
         + [index((1 - side) * deep + k, y, core) for k in range(deep)]
     )
+    load = pltpu.make_async_copy(tiles_hbm, tiles_ref, local.at[0])
+    load.start()
     z_copies, y_copies, c_copies, h_copies, x_copies = [], [], [], [], []
     for i, peer in enumerate(z_peers):
         copy = remote(own_ref, at(me), zs.at[i], zr.at[i], peer)
@@ -116,11 +116,28 @@
 
     forward(y_copies, 0, me, ys, yr, over_y)
     forward(c_copies, 0, me, cs, cr, over_core)
-    for i in range(depth):
-        copy = remote(here_ref.at[i], there_ref.at[i], hs.at[i], hr.at[i], across)
+
+    wide = here_ref.shape[0] // depth
+
+    def swap(i):
+        piece = pl.ds(i * wide, wide)
+        copy = remote(here_ref.at[piece], there_ref.at[piece], hs.at[i], hr.at[i], across)
         copy.start()
         h_copies.append(copy)
+
     batch_ref[pl.ds(me * blk, blk)] = own_ref[...]
+    picks, rows_of, marks = choose_slots(devices, blk, row_ref, col_ref, aux_ref)
+    slot_ref[0] = picks
+    slot_ref[1] = rows_of
+    m_ref[...] = marks
+    moves = [
+        pltpu.make_async_copy(slot_ref.at[0], pick_ref, local.at[1]),
+        pltpu.make_async_copy(slot_ref.at[1], at_row_ref, local.at[2]),
+    ]
+    for move in moves:
+        move.start()
+    for n in range(here_ref.shape[0] // 128):
+        here_ref[pl.ds(n * 128, 128), :] = coeffs_ref[:, pl.ds(n * 128, 128)].T
     for i in range(1, depth):
         z_copies[i - 1].wait_recv()
         dev = index((z + depth - i) % depth, y, core)
@@ -130,18 +147,23 @@
         y_copies[i].wait_recv()
         dev = index((z + depth - i) % depth, 1 - y, core)
         forward(c_copies, depth + i, dev, cs, cr, over_core)
+    for i in range(EARLY):
+        swap(i)
     for copy in c_copies:
         copy.wait_recv()
 
+    load.wait()
+    for move in moves:
+        move.wait()
     width = min(8, per)
 
     def fill(ref, j):
         def step(g, carry):
             first = j * per + g * width
             for u in range(width):
-                t = pick_ref[first + u]
+                left = batch_ref[at_row_ref[0, first + u]]
                 ref[first + u] = jnp.dot(
-                    batch_ref[row_ref[t]], tiles_ref[t], preferred_element_type=jnp.float32
+                    left, tiles_ref[pick_ref[0, first + u]], preferred_element_type=jnp.float32
                 ).astype(jnp.bfloat16)
             return carry
 
@@ -153,46 +175,56 @@
         x_copies.append(
             remote(part(send_ref, j), part(got_ref, place_at), xs.at[i], xr.at[i], peer)
         )
-        x_copies.append(remote(m_ref.at[j], m_out.at[place_at], ms.at[i], mr.at[i], peer))
+        x_copies.append(remote(m_ref, m_out.at[place_at], ms.at[i], mr.at[i], peer))
         x_copies[-2].start()
         x_copies[-1].start()
-    mine = pltpu.make_async_copy(m_ref.at[place_at], m_out.at[place_at], local.at[0])
-    mine.start()
+        if len(h_copies) < depth:
+            swap(len(h_copies))
+    m_out[place_at] = m_ref[...]
     fill(got_ref, place_at)
-    mine.wait()
     for copy in x_copies + h_copies:
         copy.wait_recv()
     for copy in z_copies + y_copies + c_copies + h_copies + x_copies:
         copy.wait_send()
 
 
-def build(tile_row, pick, own, tiles, here, marks, devices):
+def build(tile_row, tile_col, tile_aux, coeffs, tiles, devices):
     depth, half = devices // 4, devices // 2
     dma = pltpu.SemaphoreType.DMA
-    tile = tiles.shape[1]
-    slots = pick.shape[0]
+    count, tile = tiles.shape[:2]
+    rows, occupied = coeffs.shape
+    blk = rows // tile
+    slots = devices * blk * CAP
+    turned = jax.ShapeDtypeStruct((occupied, rows), coeffs.dtype)
     return pl.pallas_call(
         functools.partial(build_kernel, devices),
         out_shape=[
             jax.ShapeDtypeStruct((slots, OI, tile), jnp.bfloat16),
-            jax.ShapeDtypeStruct(marks.shape, marks.dtype),
-            jax.ShapeDtypeStruct(here.shape, here.dtype),
+            jax.ShapeDtypeStruct((half, 1, slots), jnp.int32),
+            turned,
+            turned,
         ],
-        in_specs=[SMEM, SMEM, VMEM, VMEM, VMEM, ANY],
-        out_specs=[VMEM, ANY, VMEM],
+        in_specs=[VMEM, VMEM, VMEM, VMEM, ANY],
+        out_specs=[VMEM] * 4,
         scratch_shapes=[
-            pltpu.VMEM((devices * own.shape[0],) + own.shape[1:], own.dtype),
+            pltpu.VMEM((blk, OI, tile), coeffs.dtype),
+            pltpu.VMEM(tiles.shape, tiles.dtype),
+            pltpu.VMEM((2, 1, slots), jnp.int32),
+            pltpu.VMEM((1, slots), jnp.int32),
+            pltpu.SMEM((1, slots), jnp.int32),
+            pltpu.SMEM((1, slots), jnp.int32),
+            pltpu.VMEM((devices * blk, OI, tile), coeffs.dtype),
             pltpu.VMEM((slots, OI, tile), jnp.bfloat16),
         ]
         + [dma((depth,))] * 4
         + [dma((2 * depth,))] * 2
         + [dma((depth,))] * 2
         + [dma((half,))] * 4
-        + [dma((1,))],
+        + [dma((3,))],
         compiler_params=pltpu.CompilerParams(
             collective_id=0, has_side_effects=True, vmem_limit_bytes=LIMIT
         ),
-    )(tile_row, pick, own, tiles, here, marks)
+    )(tile_row, tile_col, tile_aux, coeffs, tiles)
 
 
 def place_kernel(devices, aux_ref, got_ref, dense_ref, sums):
@@ -200,6 +232,7 @@
     blk = sums.shape[1]
     tile = got_ref.shape[2]
     side = lax.div(lax.axis_index("row"), half)
+    start = lax.rem(lax.axis_index("row"), half) * 2 * blk * CAP
     sums[...] = jnp.zeros_like(sums)
 
     def add(p, carry):
@@ -208,7 +241,7 @@
             for b in range(blk):
                 for r in range(CAP):
                     k = local + b * CAP + r
-                    a = aux_ref[p, 0, k]
+                    a = aux_ref[p, 0, start + k]
                     sums[h, b, a] += got_ref[p * 2 * blk * CAP + k].astype(jnp.float32)
         return carry
 
@@ -264,8 +297,13 @@
         b_copies.append(copy)
 
     for i, zz in enumerate(to):
-        whole = lax.dot_general(here_ref[zz], dense_ref[0], turn, preferred_element_type=f32)
-        whole += lax.dot_general(there_ref[zz], dense_ref[1], turn, preferred_element_type=f32)
+        piece = pl.ds(zz * 4 * rows, 4 * rows)
+        whole = lax.dot_general(
+            here_ref[piece, :], dense_ref[0], turn, preferred_element_type=f32
+        )
+        whole += lax.dot_general(
+            there_ref[piece, :], dense_ref[1], turn, preferred_element_type=f32
+        )
         parts[zz] = whole.astype(bf16).reshape(2, 2, rows, whole.shape[1])
         for k, yy in enumerate((1 - y, y)):
             copy = remote(
@@ -299,7 +337,7 @@
 
 def reduce(dense, here, there, devices):
     depth = devices // 4
-    rows = here.shape[1] // 4
+    rows = here.shape[0] // devices
     wide = dense.shape[1]
     dma = pltpu.SemaphoreType.DMA
 
@@ -324,12 +362,12 @@
 def on_device(devices, tiles, tile_row, tile_col, tile_aux, coeffs):
     tile = tiles.shape[1]
     rows, occupied = coeffs.shape
-    blk, depth = rows // tile, devices // 4
-    here = coeffs.T.reshape(depth, occupied // depth, rows)
-    own = coeffs[:, :OI].reshape(blk, tile, OI).transpose(0, 2, 1)
-    pick, marks = choose_slots(tile_col.reshape(-1), tile_aux, devices, blk)
-    got, got_marks, there = build(tile_row.reshape(-1), pick, own, tiles, here, marks, devices)
-    dense = place(got_marks, got, devices, blk)
+    flat = (1, tiles.shape[0])
+    got, got_marks, here, there = build(
+        tile_row.reshape(flat), tile_col.reshape(flat), tile_aux.reshape(flat),
+        coeffs, tiles, devices,
+    )
+    dense = place(got_marks, got, devices, rows // tile)
     total = reduce(dense, here, there, devices)
     return total.T.reshape(AUX, OI, occupied // devices)
 

time: 139 us -> 120 us (0.86)
  Pallas kernels: 133 us -> 114 us
    pallas_call x1, Pallas kernels: 97.7 us -> 79.3 us  [build(): pl.pallas_call(functools.partial(build_kernel, devices), out_shape=[jax.S...]
    unnamed x8 -> x10, local copies, waits for them, and re-layouts: 1.94 us -> 4.78 us
    pallas_call x1 -> x0, Pallas kernels: 2.32 us -> none  [choose_slots(): pl.pallas_call(functools.partial(slots_kernel, devices, blk), out_shape=[...]
    pallas_call x1, Pallas kernels: 29 us -> 30.7 us  [reduce(): pl.pallas_call(functools.partial(reduce_kernel, devices), out_shape=jax.S...]
    transpose x1 -> x0, local copies, waits for them, and re-layouts: 1.5 us -> none  [on_device(): here = coeffs.T.reshape(depth, occupied // depth, rows)]
where the time goes in v5:
time: 120 us
  Pallas kernels  114 us (95%)
  local copies, waits for them, and re-layouts  5.9 us (5%)
    pallas_call x1, Pallas kernels, build(): pl.pallas_call(functools.partial(build_kernel, devices), out_shape=[jax.S...  79.3 us
    pallas_call x1, Pallas kernels, reduce(): pl.pallas_call(functools.partial(reduce_kernel, devices), out_shape=jax.S...  30.7 us
    unnamed x10, local copies, waits for them, and re-layouts  4.78 us
    pallas_call x1, Pallas kernels, place(): pl.pallas_call(functools.partial(place_kernel, devices), out_shape=jax.Sh...  3.81 us

profile of v5, /device:TPU:0, one launch (start us, length us, event | category | flops | bytes accessed | tf_op | source)
XLA Modules:
  0.0 119.8 jit_solution(16898880680410658063)
XLA Ops:
  0.0 0.0 copy-start
  0.0 1.6 %copy-done = bf16[64,128,128]{2,1,0:T(8,128)(2,1)S(1)} copy-done((bf16[64,128,128]{2,1,0:T(8,128)(2,1)S(1)}, bf16[64,128,128]{2,1,0:T(8,128)(2,1)}, u32[]{:S(2)}) %copy-start) | copy-done | bytes 2097176
  1.6 0.0 copy-start.1
  1.6 1.2 %copy-done.1 = bf16[512,1024]{1,0:T(8,128)(2,1)S(1)} copy-done((bf16[512,1024]{1,0:T(8,128)(2,1)S(1)}, bf16[512,1024]{1,0:T(8,128)(2,1)}, u32[]{:S(2)}) %copy-start.1) | copy-done | bytes 1048600
  2.8 0.0 copy-start.2
  2.8 0.7 copy-done.2
  3.5 0.0 copy-start.3
  3.5 0.7 copy-done.3
  4.1 0.0 copy-start.4
  4.1 0.7 copy-done.4
  4.8 79.3 %shard_map.55 = (bf16[128,96,128]{2,1,0:T(8,128)(2,1)}, s32[8,1,128]{2,1,0:T(1,128)S(1)}, bf16[1024,512]{1,0:T(8,128)(2,1)S(1)}, bf16[1024,512]{1,0:T(8,128)(2,1)S(1)}) custom-call(s32[1,64]{1,0:T(1,128)S(1)} %bitcast.7, s32[1,64]{1,0:T(1,128)S(1)} %bitcast.8, s32[1,64]{1,0:T(1,128)S(1)} %bitcast.9, bf16[512,1024]{1,0:T(8,128)(2,1)S(1)} %copy-done.1, ...), custom_call_target="tpu_custom_call" | custom-call | tf_op jit(solution)/shard_map/pallas_call | solution.py:199
  84.1 3.8 %shard_map.56.dense_ref = bf16[2,1536,512]{2,1,0:T(8,128)(2,1)S(1)} custom-call(s32[8,1,128]{2,1,0:T(1,128)S(1)} %get-tuple-element.9.aux_ref, bf16[128,96,128]{2,1,0:T(8,128)(2,1)} %get-tuple-element.10.got_ref), custom_call_target="tpu_custom_call" | custom-call | tf_op jit(solution)/shard_map/pallas_call | solution.py:259
  88.0 30.7 %shard_map.57 = f32[64,1536]{1,0:T(8,128)S(1)} custom-call(bf16[2,1536,512]{2,1,0:T(8,128)(2,1)S(1)} %shard_map.56.dense_ref, bf16[1024,512]{1,0:T(8,128)(2,1)S(1)} %get-tuple-element.11.here_ref, bf16[1024,512]{1,0:T(8,128)(2,1)S(1)} %get-tuple-element.12.there_ref), custom_call_target="tpu_custom_call" | custom-call | tf_op jit(solution)/shard_map/pallas_call | solution.py:347
  118.7 0.2 reshape.15
  118.9 1.0 copy.6
Async XLA Ops:
  0.0 1.6 %copy-start = (bf16[64,128,128]{2,1,0:T(8,128)(2,1)S(1)}, bf16[64,128,128]{2,1,0:T(8,128)(2,1)}, u32[]{:S(2)}) copy-start(bf16[64,128,128]{2,1,0:T(8,128)(2,1)} %tiles_hbm.1) | copy-start | bytes 6291460
  1.6 1.2 %copy-start.1 = (bf16[512,1024]{1,0:T(8,128)(2,1)S(1)}, bf16[512,1024]{1,0:T(8,128)(2,1)}, u32[]{:S(2)}) copy-start(bf16[512,1024]{1,0:T(8,128)(2,1)} %coeffs_ref.1) | copy-start | bytes 3145732
  2.8 0.7 copy-start.2
  3.5 0.7 copy-start.3
  4.1 0.7 copy-start.4

commit v6 on v5

--- a/solution.py
+++ b/solution.py
@@ -15,6 +15,7 @@
 ANY = pl.BlockSpec(memory_space=pl.ANY)
 EARLY = 1
 LIMIT = 48 * 1024 * 1024
+WIDE = 60 * 1024 * 1024
 
 
 def greet(peers):
@@ -222,7 +223,7 @@
         + [dma((half,))] * 4
         + [dma((3,))],
         compiler_params=pltpu.CompilerParams(
-            collective_id=0, has_side_effects=True, vmem_limit_bytes=LIMIT
+            collective_id=0, has_side_effects=True, vmem_limit_bytes=WIDE
         ),
     )(tile_row, tile_col, tile_aux, coeffs, tiles)
 

time: 120 us -> 118 us (0.983)
  local copies, waits for them, and re-layouts: 5.9 us -> 1.8 us
  Pallas kernels: 114 us -> 116 us
    unnamed x10 -> x6, local copies, waits for them, and re-layouts: 4.78 us -> 0.67 us
    pallas_call x1, Pallas kernels: 79.3 us -> 81.1 us  [build(): pl.pallas_call(functools.partial(build_kernel, devices), out_shape=[jax.S...]
where the time goes in v6:
time: 118 us
  Pallas kernels  116 us (98%)
  local copies, waits for them, and re-layouts  1.8 us (2%)
    pallas_call x1, Pallas kernels, build(): pl.pallas_call(functools.partial(build_kernel, devices), out_shape=[jax.S...  81.1 us
    pallas_call x1, Pallas kernels, reduce(): pl.pallas_call(functools.partial(reduce_kernel, devices), out_shape=jax.S...  30.8 us
    pallas_call x1, Pallas kernels, place(): pl.pallas_call(functools.partial(place_kernel, devices), out_shape=jax.Sh...  3.95 us

profile of v6, /device:TPU:0, one launch (start us, length us, event | category | flops | bytes accessed | tf_op | source)
XLA Modules:
  0.0 117.7 jit_solution(5710615290690339165)
XLA Ops:
  0.0 81.1 %shard_map.55 = (bf16[128,96,128]{2,1,0:T(8,128)(2,1)}, s32[8,1,128]{2,1,0:T(1,128)}, bf16[1024,512]{1,0:T(8,128)(2,1)}, bf16[1024,512]{1,0:T(8,128)(2,1)}) custom-call(s32[1,64]{1,0:T(1,128)} %bitcast.7, s32[1,64]{1,0:T(1,128)} %bitcast.8, s32[1,64]{1,0:T(1,128)} %bitcast.9, bf16[512,1024]{1,0:T(8,128)(2,1)} %coeffs_ref.1, bf16[64,128,128]{2,1,0:T(8,128)(2,1)} %tiles_hbm.1), custom_call_target="tpu_custom_call" | custom-call | tf_op jit(solution)/shard_map/pallas_call | solution.py:200
  81.1 0.0 copy-start.2
  81.1 0.7 copy-done.2
  81.8 0.0 copy-start
  81.8 0.0 copy-start.1
  81.8 4.0 %shard_map.56.dense_ref = bf16[2,1536,512]{2,1,0:T(8,128)(2,1)S(1)} custom-call(s32[8,1,128]{2,1,0:T(1,128)S(1)} %copy-done.2, bf16[128,96,128]{2,1,0:T(8,128)(2,1)} %get-tuple-element.10.got_ref), custom_call_target="tpu_custom_call" | custom-call | tf_op jit(solution)/shard_map/pallas_call | solution.py:260
  85.7 0.0 copy-done
  85.8 0.0 copy-done.1
  85.8 30.8 %shard_map.57 = f32[64,1536]{1,0:T(8,128)S(1)} custom-call(bf16[2,1536,512]{2,1,0:T(8,128)(2,1)S(1)} %shard_map.56.dense_ref, bf16[1024,512]{1,0:T(8,128)(2,1)S(1)} %copy-done, bf16[1024,512]{1,0:T(8,128)(2,1)S(1)} %copy-done.1), custom_call_target="tpu_custom_call" | custom-call | tf_op jit(solution)/shard_map/pallas_call | solution.py:348
  116.5 0.2 reshape.15
  116.7 1.0 copy.6
Async XLA Ops:
  81.1 0.7 copy-start.2
  81.8 4.0 %copy-start = (bf16[1024,512]{1,0:T(8,128)(2,1)S(1)}, bf16[1024,512]{1,0:T(8,128)(2,1)}, u32[]{:S(2)}) copy-start(bf16[1024,512]{1,0:T(8,128)(2,1)} %get-tuple-element.11.here_ref) | copy-start | bytes 3145732
  81.8 4.0 %copy-start.1 = (bf16[1024,512]{1,0:T(8,128)(2,1)S(1)}, bf16[1024,512]{1,0:T(8,128)(2,1)}, u32[]{:S(2)}) copy-start(bf16[1024,512]{1,0:T(8,128)(2,1)} %get-tuple-element.12.there_ref) | copy-start | bytes 3145732
